TPU v7x, 32 devices: a whole 2x2x4 slice. The times are simulated.
32 devices in a mesh: wide: 8 (over z, x), narrow: 4 (over y, core).
Axes of the slice: x: 2, y: 2, z: 4, core: 2. Of those that a mesh axis runs over, the one named last changes fastest.
Arguments:
- latent: bfloat16 [2048, 4096], P('wide', 'narrow'), may hold values from -90 to 90
- actions: int32 [2048], P('wide'), may hold values from 0 to 255
- action_table: bfloat16 [256, 4096], P(None, 'narrow'), may hold values from -3 to 3
- norm1_gain: float32 [4096], P('narrow'), may hold values from 0.5 to 1.5
- w_query: bfloat16 [4096, 2048], P(None, 'narrow'), may hold values from -0.140625 to 0.140625
- w_key: bfloat16 [4096, 2048], P(None, 'narrow'), may hold values from -0.140625 to 0.140625
- w_value: bfloat16 [4096, 2048], P(None, 'narrow'), may hold values from -0.09375 to 0.09375
- w_out: bfloat16 [2048, 4096], P(None, 'narrow'), may hold values from -0.125 to 0.125
- key_cache: bfloat16 [16, 512, 2048], P('wide', None, 'narrow'), may hold values from -460 to 460
- value_cache: bfloat16 [16, 512, 2048], P('wide', None, 'narrow'), may hold values from -6 to 6
- norm2_gain: float32 [4096], P('narrow'), may hold values from 0.5 to 1.5
- policy_in: bfloat16 [4096, 512], P('narrow'), may hold values from -0.09375 to 0.09375
- value_in: bfloat16 [4096, 512], P('narrow'), may hold values from -0.09375 to 0.09375
- policy_out: bfloat16 [512, 256], replicated, may hold values from -12.5 to 12.5
- value_out: bfloat16 [512], replicated, may hold values from -0.25 to 0.25
- targets: int32 [2048], P('wide'), may hold values from 0 to 255
- returns: float32 [2048], P('wide'), may hold values from -19 to 19
Outputs:
- new_latent: bfloat16 [2048, 4096], P('wide', 'narrow')
- losses: float32 [2], replicated
- policy_in_grad: bfloat16 [4096, 512], P('narrow')
- value_in_grad: bfloat16 [4096, 512], P('narrow')
- policy_out_grad: bfloat16 [512, 256], replicated
- value_out_grad: bfloat16 [512], replicated
All inputs are finite; a program needn't handle non-finite values.
Results may differ from a plain program's by a relative error of at most 0.019.
Values may be sent and summed in bfloat16 or wider, within the bound.
No kernel may reach another device: no remote copies, remote signals or barrier semaphores. Data moves between devices by JAX's collectives and lax.ppermute only.
A program may use at most 64 MiB of HBM per device.

v0:
```python
import functools

import jax
import jax.numpy as jnp
from jax import lax
from jax.experimental import pallas as pl
from jax.experimental.pallas import tpu as pltpu
from jax.sharding import PartitionSpec as P

HD = 128
EPSILON = 1e-05
F32 = jnp.float32
BF16 = jnp.bfloat16
MIB = 1 << 20


def swap(block, bit):
    size = lax.axis_size("narrow")
    return lax.ppermute(block, "narrow", [(n, n ^ bit) for n in range(size)])


def far_bits():
    bit = lax.axis_size("narrow") // 2
    while bit > 1:
        yield bit
        bit //= 2


def far_blocks(block):
    blocks = {0: block}
    for bit in far_bits():
        blocks.update({d ^ bit: swap(b, bit) for d, b in list(blocks.items())})
    return blocks


def pass_blocks(blocks, *earlier):
    far = {d ^ 1: swap(after(b, *earlier), 1) for d, b in blocks.items() if d > 1}
    return {**blocks, **far}


def after(block, *earlier):
    return lax.optimization_barrier((block, *earlier))[0]


def ring_order(size):
    return list(range(0, size, 2)) + list(range(size - 1, 0, -2))


def ring_step(block, way):
    order = ring_order(lax.axis_size("wide"))
    pairs = [(a, order[(i + way) % len(order)]) for i, a in enumerate(order)]
    return lax.ppermute(block, "wide", pairs)


def next_round(pair, *earlier):
    up, down = (after(b, *earlier) for b in pair)
    return ring_step(up, 1), ring_step(down, -1)


def halves(pair, axis):
    size = pair[0].shape[axis] // 2
    return (
        lax.slice_in_dim(pair[0], 0, size, axis=axis),
        lax.slice_in_dim(pair[1], size, 2 * size, axis=axis),
    )


def dot(a, b):
    return jnp.dot(a, b, preferred_element_type=F32)


def column(row):
    return jnp.transpose(jnp.broadcast_to(row, (128, row.shape[1])))[:, :1]


def whole(shape):
    return pl.BlockSpec(shape, lambda i, p: (0,) * len(shape))


def weight_spec(ds, rows, columns):
    def at(i, p):
        d = jnp.int32(ds[0])
        for j in range(1, len(ds)):
            d = jnp.where(i == j, ds[j], d)
        return (p[0] ^ d, 0)

    return pl.BlockSpec((rows, columns), at)


def add_products(x_refs, w_refs, add):
    for step, x_ref in enumerate(x_refs):

        @pl.when(pl.program_id(0) == step)
        def _():
            for j, w_ref in enumerate(w_refs):
                add(j, dot(x_ref[...], w_ref[...]))


def project_start(count, p_ref, *refs):
    x_refs, w_refs, out = refs[:count], refs[count : count + 3], refs[-1]
    cols = w_refs[0].shape[1]

    @pl.when(pl.program_id(0) == 0)
    def _():
        out[...] = jnp.zeros_like(out)

    def add(j, product):
        out[:, j * cols : (j + 1) * cols] += product

    add_products(x_refs, w_refs, add)


def stage(ds, p_ref, *refs):
    *refs, sems = refs
    weights, caches, outs = refs[:3], refs[3:5], refs[5:]
    rows = outs[0].shape[0]
    copies = []
    for i, d in enumerate(ds):
        start = pl.multiple_of((p_ref[0] ^ d) * rows, rows)
        copies += [(w.at[pl.ds(start, rows)], outs[i * 3 + j]) for j, w in enumerate(weights)]
    copies += list(zip(caches, outs[-2:]))
    copies = [
        pltpu.make_async_copy(src, dst, sems.at[k]) for k, (src, dst) in enumerate(copies)
    ]
    for copy in copies:
        copy.start()
    for copy in copies:
        copy.wait()


def project_more(count, p_ref, acc_ref, *refs):
    x_refs, w_refs, out = refs[:count], refs[count:-1], refs[-1]
    cols = w_refs[0].shape[1]
    for j in range(3):
        at = slice(j * cols, (j + 1) * cols)
        total = acc_ref[:, at]
        for i, x_ref in enumerate(x_refs):
            total = total + dot(x_ref[...], w_refs[i * 3 + j][...])
        out[:, at] = total


def attend(count, full_width, p_ref, acc_ref, squares_ref, keys_ref, values_ref, *refs):
    project_more(count, p_ref, acc_ref, *refs[:-2], refs[-1])
    out, acc = refs[-2:]
    cols = refs[count].shape[1]
    attend_heads(full_width, cols, squares_ref, keys_ref, values_ref, out, acc)


def attend_heads(full_width, cols, squares_ref, keys_ref, values_ref, out, acc):
    scenes = keys_ref.shape[0]
    branch = acc.shape[0] // scenes
    inverse = column(lax.rsqrt(squares_ref[:1] / full_width + EPSILON))
    scaling = HD ** (-0.5)
    for s in range(scenes):
        rows = slice(s * branch, (s + 1) * branch)
        scale = inverse[rows]
        for h in range(cols // HD):
            at = slice(h * HD, (h + 1) * HD)
            q, k, v = (
                (acc[rows, j * cols + h * HD : j * cols + (h + 1) * HD] * scale).astype(BF16)
                for j in range(3)
            )
            scores = (
                lax.dot_general(
                    q,
                    keys_ref[s, :, at],
                    (((1,), (1,)), ((), ())),
                    preferred_element_type=F32,
                )
                * scaling
            )
            own = jnp.sum(q.astype(F32) * k.astype(F32), axis=1, keepdims=True) * scaling
            highest = jnp.maximum(jnp.max(scores, axis=1, keepdims=True), own)
            expd = jnp.exp(scores - highest)
            own_exp = jnp.exp(own - highest)
            total = jnp.sum(expd, axis=1, keepdims=True) + own_exp
            weights = (expd / total).astype(BF16)
            own_weight = (own_exp / total).astype(BF16)
            mixed = dot(weights, values_ref[s, :, at])
            mixed = mixed + own_weight.astype(F32) * v.astype(F32)
            out[rows, at] = mixed.astype(BF16)


def update_start(count, p_ref, tokens_ref, *refs):
    x_refs, w_ref, out = refs[:count], refs[count], refs[-1]

    @pl.when(pl.program_id(0) == 0)
    def _():
        out[...] = tokens_ref[...]

    def add(j, product):
        out[...] += product

    add_products(x_refs, [w_ref], add)


def update_end(count, p_ref, acc_ref, gain_ref, policy_ref, value_ref, *refs):
    x_refs, w_ref = refs[:count], refs[count]
    latent_out, turned_out, squares_out, keep_out, give_out, acc = refs[count + 1 :]

    @pl.when(pl.program_id(0) == 0)
    def _():
        acc[...] = acc_ref[...]

    def add(j, product):
        acc[...] += product

    add_products(x_refs, [w_ref], add)

    @pl.when(pl.program_id(0) == count - 1)
    def _():
        state = acc[...]
        latent_out[...] = state.astype(BF16)
        squares = jnp.sum(state * state, axis=1, keepdims=True)
        squares_out[...] = jnp.transpose(jnp.broadcast_to(squares, (squares.shape[0], 128)))[:8]
        gained = (state * gain_ref[...]).astype(BF16)
        turned_out[...] = jnp.transpose(gained)
        policy = dot(gained, policy_ref[...])
        value = dot(gained, value_ref[...])

        @pl.when(p_ref[0] % 2 == 0)
        def _():
            keep_out[...] = policy
            give_out[...] = value.astype(BF16)

        @pl.when(p_ref[0] % 2 == 1)
        def _():
            keep_out[...] = value
            give_out[...] = policy.astype(BF16)


def heads(full_width, total_rows, p_ref, mine_ref, theirs_ref, squares_ref, policy_out_ref,
          value_out_ref, targets_ref, returns_ref, payload_out, give_out, hidden_ref):
    inverse = column(lax.rsqrt(squares_ref[:1] / full_width + EPSILON))
    pre = (mine_ref[...].astype(F32) + theirs_ref[...].astype(F32)) * inverse
    sigma = jax.nn.sigmoid(pre)
    hidden = (pre * sigma).astype(BF16)
    hidden_ref[...] = hidden
    slope = sigma * (1.0 + pre * (1.0 - sigma)) * inverse
    factor = total_rows ** (-0.5)
    count = hidden.shape[0]
    quarter = give_out.shape[0]
    part = 4 * quarter
    at = slice(count, count + quarter)

    def put_sums(grad, loss):
        shape = (payload_out.shape[0] - count - quarter, hidden.shape[1])
        rows = lax.broadcasted_iota(jnp.int32, shape, 0)
        lanes = lax.broadcasted_iota(jnp.int32, shape, 1)
        sums = jnp.where(rows == 0, grad, 0.0)
        for lane in range(3):
            term = loss.astype(BF16).astype(F32)
            sums = jnp.where((rows == 1) & (lanes == lane), term, sums)
            loss = loss - term
        payload_out[count + quarter :] = sums.astype(BF16)

    @pl.when(p_ref[0] % 2 == 0)
    def _():
        weight = policy_out_ref[...]
        logits = dot(hidden, weight)
        top = jnp.max(logits, axis=1, keepdims=True)
        log_total = top + jnp.log(jnp.sum(jnp.exp(logits - top), axis=1, keepdims=True))
        actions = lax.broadcasted_iota(jnp.int32, logits.shape, 1).astype(F32)
        onehot = (actions == column(targets_ref[...].astype(F32))).astype(F32)
        picked = jnp.sum(logits * onehot, axis=1, keepdims=True)
        loss = jnp.sum(log_total - picked, axis=0, keepdims=True)
        dlogits = ((jnp.exp(logits - log_total) - onehot) * factor).astype(BF16)
        back = lax.dot_general(
            dlogits, weight, (((1,), (1,)), ((), ())), preferred_element_type=F32
        )
        payload_out[:count] = (back * slope).astype(BF16)
        start = pl.multiple_of((p_ref[0] // 2) * part, part)
        grad = lax.dot_general(
            hidden_ref[:, pl.ds(start, part)],
            dlogits,
            (((0,), (0,)), ((), ())),
            preferred_element_type=F32,
        ).astype(BF16)
        parts = [grad[k * quarter : (k + 1) * quarter] for k in range(4)]
        payload_out[at] = jnp.concatenate(parts[:2], axis=1)
        give_out[...] = jnp.concatenate(parts[2:], axis=1)
        put_sums(jnp.zeros((1, hidden.shape[1]), F32), loss)

    @pl.when(p_ref[0] % 2 == 1)
    def _():
        weight = value_out_ref[...].astype(F32)
        hidden_f = hidden.astype(F32)
        value = jnp.sum(hidden_f * weight, axis=1, keepdims=True)
        errors = value - column(returns_ref[...])
        loss = 0.5 * jnp.sum(errors * errors, axis=0, keepdims=True)
        dvalue = (errors * factor).astype(BF16).astype(F32)
        payload_out[:count] = (dvalue * weight * slope).astype(BF16)
        payload_out[at] = jnp.zeros_like(give_out)
        give_out[...] = jnp.zeros_like(give_out)
        put_sums(jnp.sum(dvalue * hidden_f, axis=0, keepdims=True), loss)


def sums(total_rows, p_ref, *refs):
    count = (len(refs) - 3) // 4
    share_out, losses_out, grad_out = refs[-3:]

    def total(d_refs):
        *shards, ahead, back = [ref[...].astype(F32) for ref in d_refs]
        return sum(shards, jnp.concatenate([ahead, back], axis=1))

    own, other, own_sums, other_sums = (
        total(refs[k * count : (k + 1) * count]) for k in range(4)
    )
    first = p_ref[0] % 2 == 0
    quarter = own.shape[0]
    width = share_out.shape[1]
    for k, part in enumerate((jnp.where(first, own, other), jnp.where(first, other, own))):
        for j in range(2):
            at = (2 * k + j) * quarter
            share_out[at : at + quarter] = part[:, j * width : (j + 1) * width].astype(BF16)
    policy = jnp.where(first, own_sums, other_sums)
    value = jnp.where(first, other_sums, own_sums)
    grad_out[...] = value[:1].astype(BF16)

    def loss(part):
        lanes = lax.broadcasted_iota(jnp.int32, (1, part.shape[1]), 1)
        return jnp.sum(jnp.where(lanes < 3, part[1:2], 0.0), axis=1, keepdims=True) / total_rows

    lanes = lax.broadcasted_iota(jnp.int32, (1, 2), 1)
    losses_out[...] = jnp.where(lanes == 0, loss(policy), loss(value))


def join(ds, p_ref, *refs):
    out = refs[-1]
    size = refs[0].shape[0]
    for d, ref in zip(ds, refs[:-1]):
        out[pl.ds(pl.multiple_of(((p_ref[0] ^ d) // 2) * size, size), size)] = ref[...]


def gradients(counts, p_ref, *refs):
    turned_count, count = counts
    turned, own, other = refs[:turned_count], refs[turned_count:][:count], refs[turned_count:][count:-2]
    policy_out, value_out = refs[-2:]
    upper = pl.program_id(0) < pl.num_programs(0) // 2
    *turned, ahead, back = [ref[...] for ref in turned]
    turned = jnp.concatenate([*turned, jnp.where(upper, ahead, back)], axis=1)

    def product(d_refs):
        *shards, ahead, back = [ref[...] for ref in d_refs]
        shards.append(jnp.concatenate([ahead, back], axis=1))
        return dot(turned, jnp.concatenate(shards, axis=0)).astype(BF16)

    @pl.when(p_ref[0] % 2 == 0)
    def _():
        policy_out[...] = product(own)
        value_out[...] = product(other)

    @pl.when(p_ref[0] % 2 == 1)
    def _():
        value_out[...] = product(own)
        policy_out[...] = product(other)


def call(body, name, place, steps, operands, in_specs, outs, out_specs, flops, limit, scratch=()):
    bytes_accessed = sum(x.size * x.dtype.itemsize for x in (*operands, *outs))
    return pl.pallas_call(
        body,
        name=name,
        out_shape=outs,
        grid_spec=pltpu.PrefetchScalarGridSpec(
            num_scalar_prefetch=1,
            grid=(steps,),
            in_specs=in_specs,
            out_specs=out_specs,
            scratch_shapes=scratch,
        ),
        compiler_params=pltpu.CompilerParams(
            dimension_semantics=("arbitrary",), vmem_limit_bytes=limit
        ),
        cost_estimate=pl.CostEstimate(
            flops=flops, bytes_accessed=bytes_accessed, transcendentals=0
        ),
    )(place, *operands)


def per_device(
    latent,
    actions,
    action_table,
    norm1_gain,
    w_query,
    w_key,
    w_value,
    w_out,
    key_cache,
    value_cache,
    norm2_gain,
    policy_in,
    value_in,
    policy_out,
    value_out,
    targets,
    returns,
):
    rows, width = latent.shape
    narrow_size = lax.axis_size("narrow")
    wide_size = lax.axis_size("wide")
    full_width = width * narrow_size
    cols = w_query.shape[1]
    total_rows = rows * wide_size
    action_count = action_table.shape[0]
    hidden_count = policy_in.shape[1]
    index = lax.axis_index("narrow").astype(jnp.int32)
    place = index[None]
    first = index % 2 == 0
    chips = narrow_size // 2
    near = [0, 1]
    direct = list(range(2, narrow_size, 2))
    passed = [d + 1 for d in direct]

    action_onehot = (
        actions[:, None] == jnp.arange(action_count, dtype=jnp.int32)[None, :]
    ).astype(BF16)
    tokens = latent.astype(F32) + dot(action_onehot, action_table)
    gained = (tokens * norm1_gain).astype(BF16)
    squares = jnp.sum(tokens * tokens, axis=1)
    squares = squares + swap(squares, 1)
    blocks = far_blocks(gained)
    blocks[1] = swap(gained, 1)

    weights = [pltpu.with_memory_space_constraint(w, pltpu.HBM) for w in (w_query, w_key, w_value)]

    def weight_specs(ds):
        return [weight_spec(ds, width, cols)] * 3

    acc_shape = jax.ShapeDtypeStruct((rows, 3 * cols), F32)
    acc_spec = whole((rows, 3 * cols))
    x_spec = whole((rows, width))
    flops = 2 * rows * width * 3 * cols
    acc = call(
        functools.partial(project_start, len(near)), "project_near", place, len(near),
        [*(blocks[d] for d in near), *weights],
        [*[x_spec] * len(near), *weight_specs(near)],
        [acc_shape], [acc_spec], flops * len(near), 20 * MIB,
    )[0]
    far = direct + passed
    block_shape = jax.ShapeDtypeStruct((width, cols), BF16)
    cache_shape = jax.ShapeDtypeStruct(key_cache.shape, BF16)
    outs = [block_shape] * (3 * len(far)) + [cache_shape] * 2
    anywhere = pl.BlockSpec(memory_space=pl.ANY)
    *staged, keys, values = call(
        functools.partial(stage, far), "stage", place, 1,
        [*weights, *(pltpu.with_memory_space_constraint(c, pltpu.HBM) for c in (key_cache, value_cache))],
        [anywhere] * 5, outs, [anywhere] * len(outs),
        0, 4 * MIB, [pltpu.SemaphoreType.DMA((len(outs),))],
    )
    staged_direct = staged[: 3 * len(direct)]
    staged_passed = staged[3 * len(direct) :]
    block_spec = whole((width, cols))
    blocks = pass_blocks(blocks, acc, *staged, keys, values)
    for bit in far_bits():
        squares = squares + swap(after(squares, acc), bit)
    squares = jnp.broadcast_to(squares[None, :], (8, rows))
    acc = call(
        functools.partial(project_more, len(direct)), "project_direct", place, 1,
        [acc, *(blocks[d] for d in direct), *staged_direct],
        [acc_spec, *[x_spec] * len(direct), *[block_spec] * len(staged_direct)],
        [acc_shape], [acc_spec], flops * len(direct), 24 * MIB,
    )[0]
    cache_spec = whole(key_cache.shape)
    attended = call(
        functools.partial(attend, len(passed), full_width), "attend", place, 1,
        [acc, squares, keys, values, *(blocks[d] for d in passed), *staged_passed],
        [
            acc_spec, whole(squares.shape), cache_spec, cache_spec,
            *[x_spec] * len(passed), *[block_spec] * len(staged_passed),
        ],
        [jax.ShapeDtypeStruct((rows, cols), BF16)], [whole((rows, cols))],
        flops * len(passed), 32 * MIB, [pltpu.VMEM((rows, 3 * cols), F32)],
    )[0]

    blocks = far_blocks(attended)
    blocks[1] = swap(attended, 1)
    x_spec = whole((rows, cols))
    state_spec = whole((rows, width))
    state_shape = jax.ShapeDtypeStruct((rows, width), F32)
    flops = 2 * rows * width * cols
    acc = call(
        functools.partial(update_start, len(near)), "update_near", place, len(near),
        [tokens, *(blocks[d] for d in near), w_out],
        [state_spec, *[x_spec] * len(near), weight_spec(near, cols, width)],
        [state_shape], [state_spec], flops * len(near), 16 * MIB,
    )[0]
    blocks = pass_blocks(blocks, acc)
    half = (rows, hidden_count)
    new_latent, turned, squares, keep, give = call(
        functools.partial(update_end, len(far)), "update_end", place, len(far),
        [acc, norm2_gain[None, :], policy_in, value_in, *(blocks[d] for d in far), w_out],
        [
            state_spec, whole((1, width)), whole(policy_in.shape), whole(value_in.shape),
            *[x_spec] * len(far), weight_spec(far, cols, width),
        ],
        [
            jax.ShapeDtypeStruct((rows, width), BF16),
            jax.ShapeDtypeStruct((width, rows), BF16),
            jax.ShapeDtypeStruct((8, rows), F32),
            jax.ShapeDtypeStruct(half, F32),
            jax.ShapeDtypeStruct(half, BF16),
        ],
        [state_spec, whole((width, rows)), whole((8, rows)), whole(half), whole(half)],
        flops * len(far) + 4 * rows * width * hidden_count, 32 * MIB,
        [pltpu.VMEM((rows, width), F32)],
    )
    rounds = wide_size // 2
    turned_rounds = [(turned, turned)]
    turned_rounds.append(next_round(turned_rounds[0]))

    for bit in (1, *far_bits()):
        squares = squares + swap(squares, bit)
    pre = keep + swap(give, 1).astype(F32)
    mine = pre.astype(BF16)
    *upper, last = far_bits()
    for bit in upper:
        mine = (mine.astype(F32) + swap(mine, bit).astype(F32)).astype(BF16)
    theirs = after(swap(mine, last), *turned_rounds[1])
    quarter = hidden_count // chips // 4
    payload_shape = (rows + quarter + 16, hidden_count)
    payload, give = call(
        functools.partial(heads, full_width, total_rows), "heads", place, 1,
        [
            mine, theirs, squares, policy_out, value_out[None, :], targets[None, :],
            returns[None, :],
        ],
        [
            whole(half), whole(half), whole((8, rows)), whole(policy_out.shape),
            whole((1, hidden_count)), whole((1, rows)), whole((1, rows)),
        ],
        [
            jax.ShapeDtypeStruct(payload_shape, BF16),
            jax.ShapeDtypeStruct((quarter, hidden_count), BF16),
        ],
        [whole(payload_shape), whole((quarter, hidden_count))],
        6 * rows * hidden_count * action_count, 16 * MIB, [pltpu.VMEM(half, BF16)],
    )
    taken = jnp.where(first, payload[rows : rows + quarter], swap(give, 1))
    payload = lax.dynamic_update_slice(payload, taken, (rows, 0))

    payload_rounds = [(payload, payload)]
    for step in range(1, rounds + 1):
        if step < rounds:
            ahead = turned_rounds[step] if step < rounds - 1 else halves(turned_rounds[step], 0)
            turned_rounds.append(next_round(ahead))
        ahead = payload_rounds[step - 1]
        ahead = ahead if step < rounds else halves(ahead, 1)
        payload_rounds.append(next_round(ahead, *turned_rounds[step]))
    turned_all = [turned, *(b for pair in turned_rounds[1:] for b in pair)]
    payload_own = [payload, *(b for pair in payload_rounds[1:] for b in pair)]
    payload_other = [swap(b, 1) for b in payload_own]

    pieces = [*payload_own, *payload_other]
    share_shape = (4 * quarter, action_count)
    share, losses, value_out_grad = call(
        functools.partial(sums, total_rows), "sums", place, 1, [*pieces, *pieces],
        [
            pl.BlockSpec((count, b.shape[1]), functools.partial(lambda at, i, p: (at, 0), start // count))
            for start, count in ((rows, quarter), (rows + quarter, 16))
            for b in pieces
        ],
        [
            jax.ShapeDtypeStruct(share_shape, BF16),
            jax.ShapeDtypeStruct((1, 2), F32),
            jax.ShapeDtypeStruct((1, hidden_count), BF16),
        ],
        [whole(share_shape), whole((1, 2)), whole((1, hidden_count))], 0, 8 * MIB,
    )
    losses = losses.reshape(2)
    value_out_grad = value_out_grad.reshape(hidden_count)
    shares = far_blocks(share)
    policy_out_grad = call(
        functools.partial(join, list(shares)), "join", place, 1, list(shares.values()),
        [whole(share_shape)] * len(shares),
        [jax.ShapeDtypeStruct((hidden_count, action_count), BF16)],
        [whole((hidden_count, action_count))], 0, 8 * MIB,
    )[0]

    block = 256
    half_steps = width // block // 2
    turned_specs = [pl.BlockSpec((block, rows), lambda i, p: (i, 0))] * (len(turned_all) - 2)
    turned_specs += [
        pl.BlockSpec((block, rows), lambda i, p: (jnp.minimum(i, half_steps - 1), 0)),
        pl.BlockSpec((block, rows), lambda i, p: (jnp.maximum(i - half_steps, 0), 0)),
    ]
    dpre_specs = [
        pl.BlockSpec((rows, b.shape[1]), lambda i, p: (0, 0), pipeline_mode=pl.Buffered(1))
        for b in payload_own
    ]
    grad_shape = jax.ShapeDtypeStruct((width, hidden_count), BF16)
    grad_spec = pl.BlockSpec((block, hidden_count), lambda i, p: (i, 0))
    policy_in_grad, value_in_grad = call(
        functools.partial(gradients, (len(turned_all), len(payload_own))), "gradients", place,
        width // block, [*turned_all, *payload_own, *payload_other],
        [*turned_specs, *dpre_specs, *dpre_specs],
        [grad_shape, grad_shape], [grad_spec, grad_spec],
        4 * total_rows * width * hidden_count, 28 * MIB,
    )
    return (new_latent, losses, policy_in_grad, value_in_grad, policy_out_grad, value_out_grad)


def solution(mesh):
    placed = (
        P("wide", "narrow"),
        P("wide"),
        P(None, "narrow"),
        P("narrow"),
        P(None, "narrow"),
        P(None, "narrow"),
        P(None, "narrow"),
        P(None, "narrow"),
        P("wide", None, "narrow"),
        P("wide", None, "narrow"),
        P("narrow"),
        P("narrow", None),
        P("narrow", None),
        P(),
        P(),
        P("wide"),
        P("wide"),
    )
    return jax.shard_map(
        per_device,
        mesh=mesh,
        in_specs=placed,
        out_specs=(P("wide", "narrow"), P(), P("narrow", None), P("narrow", None), P(), P()),
        check_vma=False,
    )
```

profile of v0, /device:TPU:0, one launch (start us, length us, event | category | flops | bytes accessed | tf_op | source)
XLA Modules:
  0.0 133.3 jit_solution(13164047265388585471)
XLA Ops:
  0.6 0.0 copy-start
  0.6 1.0 copy-done
  1.7 1.6 %multiply_reduce_fusion = (f32[256]{0:T(256)S(1)}, bf16[256,1024]{1,0:T(8,128)(2,1)S(1)}, f32[256,1024]{1,0:T(8,128)S(1)}) fusion(f32[1024]{0:T(1024)} %param.20, bf16[256,1024]{1,0:T(8,128)(2,1)S(1)} %copy-done, s32[256]{0:T(256)} %param.18, bf16[256,1024]{1,0:T(8,128)(2,1)} %param.17), kind=kOutput, calls=%fused_computation.1 | convolution fusion | flops 135855872 | bytes 2627584 | tf_op jit(solution)/shard_map/dot_general | solution.py:69
  3.2 0.5 collective-permute-start
  3.7 2.6 %collective-permute-start.1 = (bf16[256,1024]{1,0:T(8,128)(2,1)S(1)}, bf16[256,1024]{1,0:T(8,128)(2,1)S(1)}, u32[]{:S(2)}, u32[]{:S(2)}) collective-permute-start(bf16[256,1024]{1,0:T(8,128)(2,1)S(1)} %get-tuple-element.69.refs_0_), channel_id=1, source_target_pairs={{0,2},{1,3},{2,0},{3,1},{4,6},{5,7},{6,4},{7,5},{8,10},{9,11},{10,... | collective-permute-start | bytes 1572872 | tf_op jit(solution)/shard_map/ppermute | solution.py:19
  6.3 3.5 %stage.1 = (bf16[1024,512]{1,0:T(8,128)(2,1)S(1)}, bf16[1024,512]{1,0:T(8,128)(2,1)S(1)}, bf16[1024,512]{1,0:T(8,128)(2,1)S(1)}, bf16[1024,512]{1,0:T(8,128)(2,1...) custom-call(s32[1]{0:T(128)} %bitcast.p_ref, ...), custom_call_target="tpu_custom_call" | custom-call | bytes 23068672 | tf_op jit(solution)/shard_map/stage/pallas_call | solution.py:361
  9.8 3.9 %project_near.1.acc_ref = f32[256,1536]{1,0:T(8,128)S(1)} custom-call(s32[1]{0:T(128)} %bitcast.p_ref, bf16[256,1024]{1,0:T(8,128)(2,1)S(1)} %get-tuple-element.69.refs_0_, bf16[256,1024]{1,0:T(8,128)(2,1)S(1)} %collective-permute-done.refs_1_, bf16[4096,512]{1,0:T(8,128)(2,1)} %refs_0_.1, bf16[4096,512]{1,0:T(8,128)(2,1)} %refs_1_.1, bf16[4096,512]{1,0:T(8,128)(2,1)} %refs_2_.5), custom_call_target="tpu_custom_call" | custom-call | flops 1610612736 | bytes 15204352 | tf_op jit(solution)/shard_map/project_near/pallas_call | solution.py:361
  13.8 5.1 %collective-permute-done.1.refs_0_ = bf16[256,1024]{1,0:T(8,128)(2,1)S(1)} collective-permute-done((bf16[256,1024]{1,0:T(8,128)(2,1)S(1)}, bf16[256,1024]{1,0:T(8,128)(2,1)S(1)}, u32[]{:S(2)}, u32[]{:S(2)}) %collective-permute-start.1) | collective-permute-done | bytes 524320 | tf_op jit(solution)/shard_map/ppermute | solution.py:19
  18.9 0.5 collective-permute-start.2
  19.4 1.4 %collective-permute-done.2 = f32[256]{0:T(256)S(1)} collective-permute-done((f32[256]{0:T(256)S(1)}, f32[256]{0:T(256)S(1)}, u32[]{:S(2)}, u32[]{:S(2)}) %collective-permute-start.2) | collective-permute-done | bytes 1056 | tf_op jit(solution)/shard_map/ppermute | solution.py:19
  20.8 1.8 %collective-permute-start.3 = (f32[256]{0:T(256)S(1)}, f32[256]{0:T(256)S(1)}, u32[]{:S(2)}, u32[]{:S(2)}) collective-permute-start(f32[256]{0:T(256)S(1)} %add.23), channel_id=1, source_target_pairs={{0,2},{1,3},{2,0},{3,1},{4,6},{5,7},{6,4},{7,5},{8,10},{9,11},{10,... | collective-permute-start | bytes 3080 | tf_op jit(solution)/shard_map/ppermute | solution.py:19
  22.5 1.0 project_direct.1.acc_ref
  23.6 0.8 collective-permute-done.3
  24.4 4.0 %attend.1.refs_0_ = bf16[256,512]{1,0:T(8,128)(2,1)S(1)} custom-call(s32[1]{0:T(128)} %bitcast.p_ref, f32[256,1536]{1,0:T(8,128)S(1)} %project_direct.1.acc_ref, f32[8,256]{1,0:T(8,128)S(1)} %broadcast_in_dim.25.squares_ref, bf16[2,512,512]{2,1,0:T(8,128)(2,1)S(1)} %get-tuple-element.41.keys_ref, bf16[2,512,512]{2,1,0:T(8,128)(2,1)S(1)} %get-tuple-element.42.values_ref, ...), custom_call_target="tpu_custom_call" | custom-call | flops 805306368 | bytes 7610368 | tf_op jit(solution)/shard_map/attend/pallas_call | solution.py:361
  28.4 0.1 collective-permute-start.5
  28.5 1.8 %collective-permute-start.6 = (bf16[256,512]{1,0:T(8,128)(2,1)S(1)}, bf16[256,512]{1,0:T(8,128)(2,1)S(1)}, u32[]{:S(2)}, u32[]{:S(2)}) collective-permute-start(bf16[256,512]{1,0:T(8,128)(2,1)S(1)} %attend.1.refs_0_), channel_id=1, source_target_pairs={{0,2},{1,3},{2,0},{3,1},{4,6},{5,7},{6,4},{7,5},{8,10},{9,11},{10,... | collective-permute-start | bytes 786440 | tf_op jit(solution)/shard_map/ppermute | solution.py:19
  30.3 0.9 update_near.1.acc_ref
  31.2 5.9 %collective-permute-done.6.refs_0_ = bf16[256,512]{1,0:T(8,128)(2,1)S(1)} collective-permute-done((bf16[256,512]{1,0:T(8,128)(2,1)S(1)}, bf16[256,512]{1,0:T(8,128)(2,1)S(1)}, u32[]{:S(2)}, u32[]{:S(2)}) %collective-permute-start.6) | collective-permute-done | bytes 262176 | tf_op jit(solution)/shard_map/ppermute | solution.py:19
  37.2 1.5 %collective-permute-done.7.refs_1_ = bf16[256,512]{1,0:T(8,128)(2,1)S(1)} collective-permute-done((bf16[256,512]{1,0:T(8,128)(2,1)S(1)}, bf16[256,512]{1,0:T(8,128)(2,1)S(1)}, u32[]{:S(2)}, u32[]{:S(2)}) %collective-permute-start.7) | collective-permute-done | bytes 262176 | tf_op jit(solution)/shard_map/ppermute | solution.py:19
  38.8 2.4 %update_end.1 = (bf16[256,1024]{1,0:T(8,128)(2,1)}, bf16[1024,256]{1,0:T(8,128)(2,1)S(1)}, f32[8,256]{1,0:T(8,128)S(1)}, f32[256,512]{1,0:T(8,128)S(1)}, bf16[256,512]{1,0:T(8,128)(2,1)S(1)}) custom-call(s32[1]{0:T(128)} %bitcast.p_ref, f32[256,1024]{1,0:T(8,128)S(1)} %update_near.1.acc_ref, f32[1,1024]{1,0:T(1,128)S(1)} %bitcast.6, ...), custom_call_target="tpu_custom_call" | custom-call | flops 1073741824 | bytes 9711616 | tf_op jit(solution)/shard_map/update_end/pallas_call | solution.py:361
  41.2 0.1 collective-permute-start.8
  41.3 1.8 %collective-permute-start.10 = (bf16[1024,256]{1,0:T(8,128)(2,1)S(1)}, bf16[1024,256]{1,0:T(8,128)(2,1)S(1)}, u32[]{:S(2)}, u32[]{:S(2)}) collective-permute-start(bf16[1024,256]{1,0:T(8,128)(2,1)S(1)} %get-tuple-element.51.refs_0_), channel_id=1, source_target_pairs={{0,8},{8,16},{16,24},{24,28},{28,20},{20,12},{12,4},{4,0},{1,9},{9... | collective-permute-start | bytes 1572872 | tf_op jit(solution)/shard_map/ppermute | solution.py:52
  43.1 0.2 collective-permute-start.11
  43.4 0.1 add_convert_fusion.mine_ref
  43.4 1.8 %collective-permute-start.9 = (bf16[256,512]{1,0:T(8,128)(2,1)S(1)}, bf16[256,512]{1,0:T(8,128)(2,1)S(1)}, u32[]{:S(2)}, u32[]{:S(2)}) collective-permute-start(bf16[256,512]{1,0:T(8,128)(2,1)S(1)} %add_convert_fusion.mine_ref), channel_id=1, source_target_pairs={{0,2},{1,3},{2,0},{3,1},{4,6},{5,7},{6,4},{7,5},{8,10},{9,11},{10,... | collective-permute-start | bytes 786440 | tf_op jit(solution)/shard_map/ppermute | solution.py:19
  45.3 10.2 %collective-permute-done.10.refs_1_ = bf16[1024,256]{1,0:T(8,128)(2,1)S(1)} collective-permute-done((bf16[1024,256]{1,0:T(8,128)(2,1)S(1)}, bf16[1024,256]{1,0:T(8,128)(2,1)S(1)}, u32[]{:S(2)}, u32[]{:S(2)}) %collective-permute-start.10) | collective-permute-done | bytes 524320 | tf_op jit(solution)/shard_map/ppermute | solution.py:52
  55.5 1.8 %collective-permute-start.17 = (bf16[1024,256]{1,0:T(8,128)(2,1)S(1)}, bf16[1024,256]{1,0:T(8,128)(2,1)S(1)}, u32[]{:S(2)}, u32[]{:S(2)}) collective-permute-start(bf16[1024,256]{1,0:T(8,128)(2,1)S(1)} %collective-permute-done.10.refs_1_), channel_id=1, source_target_pairs={{0,8},{8,16},{16,24},{24,28},{28,20},{20,12},{12,4},{4,0},{1,9},{9... | collective-permute-start | bytes 1572872 | tf_op jit(solution)/shard_map/ppermute | solution.py:52
  57.3 0.2 collective-permute-start.18
  57.5 1.2 collective-permute-done.12
  58.7 1.8 %collective-permute-start.13 = (f32[8,256]{1,0:T(8,128)S(1)}, f32[8,256]{1,0:T(8,128)S(1)}, u32[]{:S(2)}, u32[]{:S(2)}) collective-permute-start(f32[8,256]{1,0:T(8,128)S(1)} %add.26), channel_id=1, source_target_pairs={{0,2},{1,3},{2,0},{3,1},{4,6},{5,7},{6,4},{7,5},{8,10},{9,11},{10,... | collective-permute-start | bytes 24584 | tf_op jit(solution)/shard_map/ppermute | solution.py:19
  60.5 1.9 %collective-permute-done.13 = f32[8,256]{1,0:T(8,128)S(1)} collective-permute-done((f32[8,256]{1,0:T(8,128)S(1)}, f32[8,256]{1,0:T(8,128)S(1)}, u32[]{:S(2)}, u32[]{:S(2)}) %collective-permute-start.13) | collective-permute-done | bytes 8224 | tf_op jit(solution)/shard_map/ppermute | solution.py:19
  62.4 1.1 heads.1
  63.5 0.1 collective-permute-start.14
  63.6 1.2 collective-permute-done.14
  64.9 1.8 %collective-permute-start.15 = (bf16[336,512]{1,0:T(8,128)(2,1)S(1)}, bf16[336,512]{1,0:T(8,128)(2,1)S(1)}, u32[]{:S(2)}, u32[]{:S(2)}) collective-permute-start(bf16[336,512]{1,0:T(8,128)(2,1)S(1)} %select_dynamic-update-slice_fusion.refs_0_.refs_18_.refs_9_), channel_id=1, source_target_pairs={{0,8},{8,16},{16,24},{24,28},{28,20},{20,12},{12,4},{4,0},{1,9},{9... | collective-permute-start | bytes 1032200 | tf_op jit(solution)/shard_map/ppermute | solution.py:52
  66.7 3.3 %collective-permute-done.17.refs_3_ = bf16[1024,256]{1,0:T(8,128)(2,1)S(1)} collective-permute-done((bf16[1024,256]{1,0:T(8,128)(2,1)S(1)}, bf16[1024,256]{1,0:T(8,128)(2,1)S(1)}, u32[]{:S(2)}, u32[]{:S(2)}) %collective-permute-start.17) | collective-permute-done | bytes 524320 | tf_op jit(solution)/shard_map/ppermute | solution.py:52
  70.0 1.8 %collective-permute-start.21 = (bf16[1024,256]{1,0:T(8,128)(2,1)S(1)}, bf16[1024,256]{1,0:T(8,128)(2,1)S(1)}, u32[]{:S(2)}, u32[]{:S(2)}) collective-permute-start(bf16[1024,256]{1,0:T(8,128)(2,1)S(1)} %collective-permute-done.17.refs_3_), channel_id=1, source_target_pairs={{0,8},{8,16},{16,24},{24,28},{28,20},{20,12},{12,4},{4,0},{1,9},{9... | collective-permute-start | bytes 1572872 | tf_op jit(solution)/shard_map/ppermute | solution.py:52
  71.8 0.2 collective-permute-start.22
  72.0 1.7 %collective-permute-start.16 = (bf16[336,512]{1,0:T(8,128)(2,1)S(1)}, bf16[336,512]{1,0:T(8,128)(2,1)S(1)}, u32[]{:S(2)}, u32[]{:S(2)}) collective-permute-start(bf16[336,512]{1,0:T(8,128)(2,1)S(1)} %select_dynamic-update-slice_fusion.refs_0_.refs_18_.refs_9_), channel_id=1, source_target_pairs={{0,4},{8,0},{16,8},{24,16},{28,24},{20,28},{12,20},{4,12},{1,5},{9... | collective-permute-start | bytes 1032200 | tf_op jit(solution)/shard_map/ppermute | solution.py:52
  73.8 3.6 %collective-permute-done.15.refs_1_.refs_19_.refs_10_ = bf16[336,512]{1,0:T(8,128)(2,1)S(1)} collective-permute-done((bf16[336,512]{1,0:T(8,128)(2,1)S(1)}, bf16[336,512]{1,0:T(8,128)(2,1)S(1)}, u32[]{:S(2)}, u32[]{:S(2)}) %collective-permute-start.15) | collective-permute-done | bytes 344096 | tf_op jit(solution)/shard_map/ppermute | solution.py:52
  77.4 1.8 %collective-permute-start.19 = (bf16[336,512]{1,0:T(8,128)(2,1)S(1)}, bf16[336,512]{1,0:T(8,128)(2,1)S(1)}, u32[]{:S(2)}, u32[]{:S(2)}) collective-permute-start(bf16[336,512]{1,0:T(8,128)(2,1)S(1)} %collective-permute-done.15.refs_1_.refs_19_.refs_10_), channel_id=1, source_target_pairs={{0,8},{8,16},{16,24},{24,28},{28,20},{20,12},{12,4},{4,0},{1,9},{9... | collective-permute-start | bytes 1032200 | tf_op jit(solution)/shard_map/ppermute | solution.py:52
  79.2 12.3 %collective-permute-done.16.refs_2_.refs_20_.refs_11_ = bf16[336,512]{1,0:T(8,128)(2,1)S(1)} collective-permute-done((bf16[336,512]{1,0:T(8,128)(2,1)S(1)}, bf16[336,512]{1,0:T(8,128)(2,1)S(1)}, u32[]{:S(2)}, u32[]{:S(2)}) %collective-permute-start.16) | collective-permute-done | bytes 344096 | tf_op jit(solution)/shard_map/ppermute | solution.py:52
  91.5 0.2 collective-permute-start.20
  91.7 3.1 %collective-permute-done.19.refs_3_.refs_21_.refs_12_ = bf16[336,512]{1,0:T(8,128)(2,1)S(1)} collective-permute-done((bf16[336,512]{1,0:T(8,128)(2,1)S(1)}, bf16[336,512]{1,0:T(8,128)(2,1)S(1)}, u32[]{:S(2)}, u32[]{:S(2)}) %collective-permute-start.19) | collective-permute-done | bytes 344096 | tf_op jit(solution)/shard_map/ppermute | solution.py:52
  94.9 1.8 %collective-permute-start.23 = (bf16[336,512]{1,0:T(8,128)(2,1)S(1)}, bf16[336,512]{1,0:T(8,128)(2,1)S(1)}, u32[]{:S(2)}, u32[]{:S(2)}) collective-permute-start(bf16[336,512]{1,0:T(8,128)(2,1)S(1)} %collective-permute-done.19.refs_3_.refs_21_.refs_12_), channel_id=1, source_target_pairs={{0,8},{8,16},{16,24},{24,28},{28,20},{20,12},{12,4},{4,0},{1,9},{9... | collective-permute-start | bytes 1032200 | tf_op jit(solution)/shard_map/ppermute | solution.py:52
  96.7 1.6 %collective-permute-start.25 = (bf16[512,256]{1,0:T(8,128)(2,1)S(1)}, bf16[512,256]{1,0:T(8,128)(2,1)S(1)}, u32[]{:S(2)}, u32[]{:S(2)}) collective-permute-start(bf16[512,256]{1,0:T(8,128)(2,1)S(1)} %slice.21), channel_id=1, source_target_pairs={{0,8},{8,16},{16,24},{24,28},{28,20},{20,12},{12,4},{4,0},{1,9},{9... | collective-permute-start | bytes 786440 | tf_op jit(solution)/shard_map/ppermute | solution.py:52
  98.4 0.5 collective-permute-start.26
  98.9 0.2 collective-permute-start.24
  99.1 10.4 %collective-permute-done.25.refs_7_ = bf16[512,256]{1,0:T(8,128)(2,1)S(1)} collective-permute-done((bf16[512,256]{1,0:T(8,128)(2,1)S(1)}, bf16[512,256]{1,0:T(8,128)(2,1)S(1)}, u32[]{:S(2)}, u32[]{:S(2)}) %collective-permute-start.25) | collective-permute-done | bytes 262176 | tf_op jit(solution)/shard_map/ppermute | solution.py:52
  109.4 0.5 collective-permute-start.31
  110.0 0.1 collective-permute-start.32
  110.0 2.4 %collective-permute-done.24.refs_6_.refs_24_.refs_15_ = bf16[336,512]{1,0:T(8,128)(2,1)S(1)} collective-permute-done((bf16[336,512]{1,0:T(8,128)(2,1)S(1)}, bf16[336,512]{1,0:T(8,128)(2,1)S(1)}, u32[]{:S(2)}, u32[]{:S(2)}) %collective-permute-start.24) | collective-permute-done | bytes 344096 | tf_op jit(solution)/shard_map/ppermute | solution.py:52
  112.4 1.6 %collective-permute-start.27 = (bf16[336,256]{1,0:T(8,128)(2,1)S(1)}, bf16[336,256]{1,0:T(8,128)(2,1)S(1)}, u32[]{:S(2)}, u32[]{:S(2)}) collective-permute-start(bf16[336,256]{1,0:T(8,128)(2,1)S(1)} %slice.20), channel_id=1, source_target_pairs={{0,8},{8,16},{16,24},{24,28},{28,20},{20,12},{12,4},{4,0},{1,9},{9... | collective-permute-start | bytes 516104 | tf_op jit(solution)/shard_map/ppermute | solution.py:52
  114.1 0.2 collective-permute-start.34
  114.3 0.3 collective-permute-start.35
  114.6 0.4 collective-permute-start.28
  115.0 4.2 %collective-permute-done.27.refs_7_.refs_25_.refs_16_ = bf16[336,256]{1,0:T(8,128)(2,1)S(1)} collective-permute-done((bf16[336,256]{1,0:T(8,128)(2,1)S(1)}, bf16[336,256]{1,0:T(8,128)(2,1)S(1)}, u32[]{:S(2)}, u32[]{:S(2)}) %collective-permute-start.27) | collective-permute-done | bytes 172064 | tf_op jit(solution)/shard_map/ppermute | solution.py:52
  119.3 1.8 %collective-permute-done.28.refs_8_.refs_26_.refs_17_ = bf16[336,256]{1,0:T(8,128)(2,1)S(1)} collective-permute-done((bf16[336,256]{1,0:T(8,128)(2,1)S(1)}, bf16[336,256]{1,0:T(8,128)(2,1)S(1)}, u32[]{:S(2)}, u32[]{:S(2)}) %collective-permute-start.28) | collective-permute-done | bytes 172064 | tf_op jit(solution)/shard_map/ppermute | solution.py:52
  121.1 1.4 %collective-permute-done.37.refs_17_.refs_35_.refs_26_ = bf16[336,256]{1,0:T(8,128)(2,1)S(1)} collective-permute-done((bf16[336,256]{1,0:T(8,128)(2,1)S(1)}, bf16[336,256]{1,0:T(8,128)(2,1)S(1)}, u32[]{:S(2)}, u32[]{:S(2)}) %collective-permute-start.37) | collective-permute-done | bytes 172064 | tf_op jit(solution)/shard_map/ppermute | solution.py:19
  122.5 0.7 sums.1
  123.2 1.5 %collective-permute-start.38 = (bf16[256,256]{1,0:T(8,128)(2,1)S(1)}, bf16[256,256]{1,0:T(8,128)(2,1)S(1)}, u32[]{:S(2)}, u32[]{:S(2)}) collective-permute-start(bf16[256,256]{1,0:T(8,128)(2,1)S(1)} %get-tuple-element.66.refs_0_), channel_id=1, source_target_pairs={{0,2},{1,3},{2,0},{3,1},{4,6},{5,7},{6,4},{7,5},{8,10},{9,11},{10,... | collective-permute-start | bytes 393224 | tf_op jit(solution)/shard_map/ppermute | solution.py:19
  124.8 7.2 %gradients.1 = (bf16[1024,512]{1,0:T(8,128)(2,1)}, bf16[1024,512]{1,0:T(8,128)(2,1)}) custom-call(s32[1]{0:T(128)} %bitcast.p_ref, bf16[1024,256]{1,0:T(8,128)(2,1)S(1)} %get-tuple-element.51.refs_0_, bf16[1024,256]{1,0:T(8,128)(2,1)S(1)} %collective-permute-done.10.refs_1_, bf16[1024,256]{1,0:T(8,128)(2,1)S(1)} %collective-permute-done.11.refs_2_, ...), custom_call_target="tpu_custom_call" | custom-call | flops 4294967296 | bytes 11796480 | tf_op jit(solution)/shard_map/gradients/pallas_call | solution.py:361
  131.9 0.6 reduce
  132.5 0.7 join.1
  (56 shorter events, 0.2 us)
Async XLA Ops:
  0.6 1.0 copy-start
  3.2 6.6 %collective-permute-start = (bf16[256,1024]{1,0:T(8,128)(2,1)S(1)}, bf16[256,1024]{1,0:T(8,128)(2,1)S(1)}, u32[]{:S(2)}, u32[]{:S(2)}) collective-permute-start(bf16[256,1024]{1,0:T(8,128)(2,1)S(1)} %get-tuple-element.69.refs_0_), channel_id=1, source_target_pairs={{0,1},{1,0},{2,3},{3,2},{4,5},{5,4},{6,7},{7,6},{8,9},{9,8},{10,11... | collective-permute-start | bytes 1572872 | tf_op jit(solution)/shard_map/ppermute | solution.py:19
  3.7 15.1 %collective-permute-start.1 = (bf16[256,1024]{1,0:T(8,128)(2,1)S(1)}, bf16[256,1024]{1,0:T(8,128)(2,1)S(1)}, u32[]{:S(2)}, u32[]{:S(2)}) collective-permute-start(bf16[256,1024]{1,0:T(8,128)(2,1)S(1)} %get-tuple-element.69.refs_0_), channel_id=1, source_target_pairs={{0,2},{1,3},{2,0},{3,1},{4,6},{5,7},{6,4},{7,5},{8,10},{9,11},{10,... | collective-permute-start | bytes 1572872 | tf_op jit(solution)/shard_map/ppermute | solution.py:19
  18.9 5.5 %collective-permute-start.4 = (bf16[256,1024]{1,0:T(8,128)(2,1)S(1)}, bf16[256,1024]{1,0:T(8,128)(2,1)S(1)}, u32[]{:S(2)}, u32[]{:S(2)}) collective-permute-start(bf16[256,1024]{1,0:T(8,128)(2,1)S(1)} %collective-permute-done.1.refs_0_), channel_id=1, source_target_pairs={{0,1},{1,0},{2,3},{3,2},{4,5},{5,4},{6,7},{7,6},{8,9},{9,8},{10,11... | collective-permute-start | bytes 1572872 | tf_op jit(solution)/shard_map/ppermute | solution.py:19
  18.9 1.9 %collective-permute-start.2 = (f32[256]{0:T(256)S(1)}, f32[256]{0:T(256)S(1)}, u32[]{:S(2)}, u32[]{:S(2)}) collective-permute-start(f32[256]{0:T(256)S(1)} %get-tuple-element.68), channel_id=1, source_target_pairs={{0,1},{1,0},{2,3},{3,2},{4,5},{5,4},{6,7},{7,6},{8,9},{9,8},{10,11... | collective-permute-start | bytes 3080 | tf_op jit(solution)/shard_map/ppermute | solution.py:19
  20.8 3.6 %collective-permute-start.3 = (f32[256]{0:T(256)S(1)}, f32[256]{0:T(256)S(1)}, u32[]{:S(2)}, u32[]{:S(2)}) collective-permute-start(f32[256]{0:T(256)S(1)} %add.23), channel_id=1, source_target_pairs={{0,2},{1,3},{2,0},{3,1},{4,6},{5,7},{6,4},{7,5},{8,10},{9,11},{10,... | collective-permute-start | bytes 3080 | tf_op jit(solution)/shard_map/ppermute | solution.py:19
  23.5 6.8 %copy-start.1 = (bf16[2048,1024]{1,0:T(8,128)(2,1)S(1)}, bf16[2048,1024]{1,0:T(8,128)(2,1)}, u32[]{:S(2)}) copy-start(bf16[2048,1024]{1,0:T(8,128)(2,1)} %refs_2_.7) | copy-start | bytes 12582916
  28.4 10.4 %copy-start.2 = (bf16[1024,512]{1,0:T(8,128)(2,1)S(1)}, bf16[1024,512]{1,0:T(8,128)(2,1)}, u32[]{:S(2)}) copy-start(bf16[1024,512]{1,0:T(8,128)(2,1)} %policy_ref.1) | copy-start | bytes 3145732
  28.4 10.4 %copy-start.3 = (bf16[1024,512]{1,0:T(8,128)(2,1)S(1)}, bf16[1024,512]{1,0:T(8,128)(2,1)}, u32[]{:S(2)}) copy-start(bf16[1024,512]{1,0:T(8,128)(2,1)} %value_ref.1) | copy-start | bytes 3145732
  28.4 10.4 %copy-start.5 = (f32[1024]{0:T(1024)S(1)}, f32[1024]{0:T(1024)}, u32[]{:S(2)}) copy-start(f32[1024]{0:T(1024)} %param.27) | copy-start | bytes 12292
  28.4 1.9 %collective-permute-start.5 = (bf16[256,512]{1,0:T(8,128)(2,1)S(1)}, bf16[256,512]{1,0:T(8,128)(2,1)S(1)}, u32[]{:S(2)}, u32[]{:S(2)}) collective-permute-start(bf16[256,512]{1,0:T(8,128)(2,1)S(1)} %attend.1.refs_0_), channel_id=1, source_target_pairs={{0,1},{1,0},{2,3},{3,2},{4,5},{5,4},{6,7},{7,6},{8,9},{9,8},{10,11... | collective-permute-start | bytes 786440 | tf_op jit(solution)/shard_map/ppermute | solution.py:19
  28.5 8.7 %collective-permute-start.6 = (bf16[256,512]{1,0:T(8,128)(2,1)S(1)}, bf16[256,512]{1,0:T(8,128)(2,1)S(1)}, u32[]{:S(2)}, u32[]{:S(2)}) collective-permute-start(bf16[256,512]{1,0:T(8,128)(2,1)S(1)} %attend.1.refs_0_), channel_id=1, source_target_pairs={{0,2},{1,3},{2,0},{3,1},{4,6},{5,7},{6,4},{7,5},{8,10},{9,11},{10,... | collective-permute-start | bytes 786440 | tf_op jit(solution)/shard_map/ppermute | solution.py:19
  37.2 1.5 %collective-permute-start.7 = (bf16[256,512]{1,0:T(8,128)(2,1)S(1)}, bf16[256,512]{1,0:T(8,128)(2,1)S(1)}, u32[]{:S(2)}, u32[]{:S(2)}) collective-permute-start(bf16[256,512]{1,0:T(8,128)(2,1)S(1)} %collective-permute-done.6.refs_0_), channel_id=1, source_target_pairs={{0,1},{1,0},{2,3},{3,2},{4,5},{5,4},{6,7},{7,6},{8,9},{9,8},{10,11... | collective-permute-start | bytes 786440 | tf_op jit(solution)/shard_map/ppermute | solution.py:19
  38.7 21.7 %copy-start.8 = (bf16[512]{0:T(512)(128)(2,1)S(1)}, bf16[512]{0:T(512)(128)(2,1)}, u32[]{:S(2)}) copy-start(bf16[512]{0:T(512)(128)(2,1)} %param.31) | copy-start | bytes 3076
  38.8 23.6 %copy-start.4 = (bf16[512,256]{1,0:T(8,128)(2,1)S(1)}, bf16[512,256]{1,0:T(8,128)(2,1)}, u32[]{:S(2)}) copy-start(bf16[512,256]{1,0:T(8,128)(2,1)} %policy_out_ref.1) | copy-start | bytes 786436
  38.8 23.6 %copy-start.6 = (s32[256]{0:T(256)S(1)}, s32[256]{0:T(256)}, u32[]{:S(2)}) copy-start(s32[256]{0:T(256)} %param.32) | copy-start | bytes 3076
  38.8 23.6 %copy-start.7 = (f32[256]{0:T(256)S(1)}, f32[256]{0:T(256)}, u32[]{:S(2)}) copy-start(f32[256]{0:T(256)} %param.33) | copy-start | bytes 3076
  41.2 2.2 %collective-permute-start.8 = (bf16[256,512]{1,0:T(8,128)(2,1)S(1)}, bf16[256,512]{1,0:T(8,128)(2,1)S(1)}, u32[]{:S(2)}, u32[]{:S(2)}) collective-permute-start(bf16[256,512]{1,0:T(8,128)(2,1)S(1)} %get-tuple-element.50), channel_id=1, source_target_pairs={{0,1},{1,0},{2,3},{3,2},{4,5},{5,4},{6,7},{7,6},{8,9},{9,8},{10,11... | collective-permute-start | bytes 786440 | tf_op jit(solution)/shard_map/ppermute | solution.py:19
  41.3 14.2 %collective-permute-start.10 = (bf16[1024,256]{1,0:T(8,128)(2,1)S(1)}, bf16[1024,256]{1,0:T(8,128)(2,1)S(1)}, u32[]{:S(2)}, u32[]{:S(2)}) collective-permute-start(bf16[1024,256]{1,0:T(8,128)(2,1)S(1)} %get-tuple-element.51.refs_0_), channel_id=1, source_target_pairs={{0,8},{8,16},{16,24},{24,28},{28,20},{20,12},{12,4},{4,0},{1,9},{9... | collective-permute-start | bytes 1572872 | tf_op jit(solution)/shard_map/ppermute | solution.py:52
  43.1 14.2 %collective-permute-start.11 = (bf16[1024,256]{1,0:T(8,128)(2,1)S(1)}, bf16[1024,256]{1,0:T(8,128)(2,1)S(1)}, u32[]{:S(2)}, u32[]{:S(2)}) collective-permute-start(bf16[1024,256]{1,0:T(8,128)(2,1)S(1)} %get-tuple-element.51.refs_0_), channel_id=1, source_target_pairs={{0,4},{8,0},{16,8},{24,16},{28,24},{20,28},{12,20},{4,12},{1,5},{9... | collective-permute-start | bytes 1572872 | tf_op jit(solution)/shard_map/ppermute | solution.py:52
  43.4 18.9 %collective-permute-start.9 = (bf16[256,512]{1,0:T(8,128)(2,1)S(1)}, bf16[256,512]{1,0:T(8,128)(2,1)S(1)}, u32[]{:S(2)}, u32[]{:S(2)}) collective-permute-start(bf16[256,512]{1,0:T(8,128)(2,1)S(1)} %add_convert_fusion.mine_ref), channel_id=1, source_target_pairs={{0,2},{1,3},{2,0},{3,1},{4,6},{5,7},{6,4},{7,5},{8,10},{9,11},{10,... | collective-permute-start | bytes 786440 | tf_op jit(solution)/shard_map/ppermute | solution.py:19
  55.5 14.5 %collective-permute-start.17 = (bf16[1024,256]{1,0:T(8,128)(2,1)S(1)}, bf16[1024,256]{1,0:T(8,128)(2,1)S(1)}, u32[]{:S(2)}, u32[]{:S(2)}) collective-permute-start(bf16[1024,256]{1,0:T(8,128)(2,1)S(1)} %collective-permute-done.10.refs_1_), channel_id=1, source_target_pairs={{0,8},{8,16},{16,24},{24,28},{28,20},{20,12},{12,4},{4,0},{1,9},{9... | collective-permute-start | bytes 1572872 | tf_op jit(solution)/shard_map/ppermute | solution.py:52
  57.3 14.5 %collective-permute-start.18 = (bf16[1024,256]{1,0:T(8,128)(2,1)S(1)}, bf16[1024,256]{1,0:T(8,128)(2,1)}, u32[]{:S(2)}, u32[]{:S(2)}) collective-permute-start(bf16[1024,256]{1,0:T(8,128)(2,1)S(1)} %collective-permute-done.11.refs_2_), channel_id=1, source_target_pairs={{0,4},{8,0},{16,8},{24,16},{28,24},{20,28},{12,20},{4,12},{1,5},{9... | collective-permute-start | bytes 1572872 | tf_op jit(solution)/shard_map/ppermute | solution.py:52
  57.5 1.2 collective-permute-start.12
  58.7 3.7 %collective-permute-start.13 = (f32[8,256]{1,0:T(8,128)S(1)}, f32[8,256]{1,0:T(8,128)S(1)}, u32[]{:S(2)}, u32[]{:S(2)}) collective-permute-start(f32[8,256]{1,0:T(8,128)S(1)} %add.26), channel_id=1, source_target_pairs={{0,2},{1,3},{2,0},{3,1},{4,6},{5,7},{6,4},{7,5},{8,10},{9,11},{10,... | collective-permute-start | bytes 24584 | tf_op jit(solution)/shard_map/ppermute | solution.py:19
  63.5 1.3 collective-permute-start.14
  64.9 12.5 %collective-permute-start.15 = (bf16[336,512]{1,0:T(8,128)(2,1)S(1)}, bf16[336,512]{1,0:T(8,128)(2,1)S(1)}, u32[]{:S(2)}, u32[]{:S(2)}) collective-permute-start(bf16[336,512]{1,0:T(8,128)(2,1)S(1)} %select_dynamic-update-slice_fusion.refs_0_.refs_18_.refs_9_), channel_id=1, source_target_pairs={{0,8},{8,16},{16,24},{24,28},{28,20},{20,12},{12,4},{4,0},{1,9},{9... | collective-permute-start | bytes 1032200 | tf_op jit(solution)/shard_map/ppermute | solution.py:52
  70.0 24.9 %collective-permute-start.21 = (bf16[1024,256]{1,0:T(8,128)(2,1)S(1)}, bf16[1024,256]{1,0:T(8,128)(2,1)S(1)}, u32[]{:S(2)}, u32[]{:S(2)}) collective-permute-start(bf16[1024,256]{1,0:T(8,128)(2,1)S(1)} %collective-permute-done.17.refs_3_), channel_id=1, source_target_pairs={{0,8},{8,16},{16,24},{24,28},{28,20},{20,12},{12,4},{4,0},{1,9},{9... | collective-permute-start | bytes 1572872 | tf_op jit(solution)/shard_map/ppermute | solution.py:52
  71.8 23.1 %collective-permute-start.22 = (bf16[1024,256]{1,0:T(8,128)(2,1)}, bf16[1024,256]{1,0:T(8,128)(2,1)S(1)}, u32[]{:S(2)}, u32[]{:S(2)}) collective-permute-start(bf16[1024,256]{1,0:T(8,128)(2,1)} %collective-permute-done.18.refs_4_), channel_id=1, source_target_pairs={{0,4},{8,0},{16,8},{24,16},{28,24},{20,28},{12,20},{4,12},{1,5},{9... | collective-permute-start | bytes 1572872 | tf_op jit(solution)/shard_map/ppermute | solution.py:52
  72.0 19.5 %collective-permute-start.16 = (bf16[336,512]{1,0:T(8,128)(2,1)S(1)}, bf16[336,512]{1,0:T(8,128)(2,1)S(1)}, u32[]{:S(2)}, u32[]{:S(2)}) collective-permute-start(bf16[336,512]{1,0:T(8,128)(2,1)S(1)} %select_dynamic-update-slice_fusion.refs_0_.refs_18_.refs_9_), channel_id=1, source_target_pairs={{0,4},{8,0},{16,8},{24,16},{28,24},{20,28},{12,20},{4,12},{1,5},{9... | collective-permute-start | bytes 1032200 | tf_op jit(solution)/shard_map/ppermute | solution.py:52
  77.4 17.5 %collective-permute-start.19 = (bf16[336,512]{1,0:T(8,128)(2,1)S(1)}, bf16[336,512]{1,0:T(8,128)(2,1)S(1)}, u32[]{:S(2)}, u32[]{:S(2)}) collective-permute-start(bf16[336,512]{1,0:T(8,128)(2,1)S(1)} %collective-permute-done.15.refs_1_.refs_19_.refs_10_), channel_id=1, source_target_pairs={{0,8},{8,16},{16,24},{24,28},{28,20},{20,12},{12,4},{4,0},{1,9},{9... | collective-permute-start | bytes 1032200 | tf_op jit(solution)/shard_map/ppermute | solution.py:52
  91.5 7.4 %collective-permute-start.20 = (bf16[336,512]{1,0:T(8,128)(2,1)S(1)}, bf16[336,512]{1,0:T(8,128)(2,1)S(1)}, u32[]{:S(2)}, u32[]{:S(2)}) collective-permute-start(bf16[336,512]{1,0:T(8,128)(2,1)S(1)} %collective-permute-done.16.refs_2_.refs_20_.refs_11_), channel_id=1, source_target_pairs={{0,4},{8,0},{16,8},{24,16},{28,24},{20,28},{12,20},{4,12},{1,5},{9... | collective-permute-start | bytes 1032200 | tf_op jit(solution)/shard_map/ppermute | solution.py:52
  94.9 15.1 %collective-permute-start.23 = (bf16[336,512]{1,0:T(8,128)(2,1)S(1)}, bf16[336,512]{1,0:T(8,128)(2,1)S(1)}, u32[]{:S(2)}, u32[]{:S(2)}) collective-permute-start(bf16[336,512]{1,0:T(8,128)(2,1)S(1)} %collective-permute-done.19.refs_3_.refs_21_.refs_12_), channel_id=1, source_target_pairs={{0,8},{8,16},{16,24},{24,28},{28,20},{20,12},{12,4},{4,0},{1,9},{9... | collective-permute-start | bytes 1032200 | tf_op jit(solution)/shard_map/ppermute | solution.py:52
  96.7 12.7 %collective-permute-start.25 = (bf16[512,256]{1,0:T(8,128)(2,1)S(1)}, bf16[512,256]{1,0:T(8,128)(2,1)S(1)}, u32[]{:S(2)}, u32[]{:S(2)}) collective-permute-start(bf16[512,256]{1,0:T(8,128)(2,1)S(1)} %slice.21), channel_id=1, source_target_pairs={{0,8},{8,16},{16,24},{24,28},{28,20},{20,12},{12,4},{4,0},{1,9},{9... | collective-permute-start | bytes 786440 | tf_op jit(solution)/shard_map/ppermute | solution.py:52
  98.4 11.1 %collective-permute-start.26 = (bf16[512,256]{1,0:T(8,128)(2,1)S(1)}, bf16[512,256]{1,0:T(8,128)(2,1)S(1)}, u32[]{:S(2)}, u32[]{:S(2)}) collective-permute-start(bf16[512,256]{1,0:T(8,128)(2,1)S(1)} %slice.22), channel_id=1, source_target_pairs={{0,4},{8,0},{16,8},{24,16},{28,24},{20,28},{12,20},{4,12},{1,5},{9... | collective-permute-start | bytes 786440 | tf_op jit(solution)/shard_map/ppermute | solution.py:52
  98.9 13.5 %collective-permute-start.24 = (bf16[336,512]{1,0:T(8,128)(2,1)S(1)}, bf16[336,512]{1,0:T(8,128)(2,1)S(1)}, u32[]{:S(2)}, u32[]{:S(2)}) collective-permute-start(bf16[336,512]{1,0:T(8,128)(2,1)S(1)} %collective-permute-done.20.refs_4_.refs_22_.refs_13_), channel_id=1, source_target_pairs={{0,4},{8,0},{16,8},{24,16},{28,24},{20,28},{12,20},{4,12},{1,5},{9... | collective-permute-start | bytes 1032200 | tf_op jit(solution)/shard_map/ppermute | solution.py:52
  99.1 13.4 %collective-permute-start.29 = (bf16[336,512]{1,0:T(8,128)(2,1)S(1)}, bf16[336,512]{1,0:T(8,128)(2,1)S(1)}, u32[]{:S(2)}, u32[]{:S(2)}) collective-permute-start(bf16[336,512]{1,0:T(8,128)(2,1)S(1)} %select_dynamic-update-slice_fusion.refs_0_.refs_18_.refs_9_), channel_id=1, source_target_pairs={{0,1},{1,0},{2,3},{3,2},{4,5},{5,4},{6,7},{7,6},{8,9},{9,8},{10,11... | collective-permute-start | bytes 1032200 | tf_op jit(solution)/shard_map/ppermute | solution.py:19
  109.4 4.6 %collective-permute-start.30 = (bf16[336,512]{1,0:T(8,128)(2,1)S(1)}, bf16[336,512]{1,0:T(8,128)(2,1)S(1)}, u32[]{:S(2)}, u32[]{:S(2)}) collective-permute-start(bf16[336,512]{1,0:T(8,128)(2,1)S(1)} %collective-permute-done.15.refs_1_.refs_19_.refs_10_), channel_id=1, source_target_pairs={{0,1},{1,0},{2,3},{3,2},{4,5},{5,4},{6,7},{7,6},{8,9},{9,8},{10,11... | collective-permute-start | bytes 1032200 | tf_op jit(solution)/shard_map/ppermute | solution.py:19
  109.4 4.9 %collective-permute-start.31 = (bf16[336,512]{1,0:T(8,128)(2,1)S(1)}, bf16[336,512]{1,0:T(8,128)(2,1)S(1)}, u32[]{:S(2)}, u32[]{:S(2)}) collective-permute-start(bf16[336,512]{1,0:T(8,128)(2,1)S(1)} %collective-permute-done.16.refs_2_.refs_20_.refs_11_), channel_id=1, source_target_pairs={{0,1},{1,0},{2,3},{3,2},{4,5},{5,4},{6,7},{7,6},{8,9},{9,8},{10,11... | collective-permute-start | bytes 1032200 | tf_op jit(solution)/shard_map/ppermute | solution.py:19
  110.0 4.6 %collective-permute-start.32 = (bf16[336,512]{1,0:T(8,128)(2,1)S(1)}, bf16[336,512]{1,0:T(8,128)(2,1)S(1)}, u32[]{:S(2)}, u32[]{:S(2)}) collective-permute-start(bf16[336,512]{1,0:T(8,128)(2,1)S(1)} %collective-permute-done.19.refs_3_.refs_21_.refs_12_), channel_id=1, source_target_pairs={{0,1},{1,0},{2,3},{3,2},{4,5},{5,4},{6,7},{7,6},{8,9},{9,8},{10,11... | collective-permute-start | bytes 1032200 | tf_op jit(solution)/shard_map/ppermute | solution.py:19
  112.4 8.7 %collective-permute-start.33 = (bf16[336,512]{1,0:T(8,128)(2,1)S(1)}, bf16[336,512]{1,0:T(8,128)(2,1)S(1)}, u32[]{:S(2)}, u32[]{:S(2)}) collective-permute-start(bf16[336,512]{1,0:T(8,128)(2,1)S(1)} %collective-permute-done.20.refs_4_.refs_22_.refs_13_), channel_id=1, source_target_pairs={{0,1},{1,0},{2,3},{3,2},{4,5},{5,4},{6,7},{7,6},{8,9},{9,8},{10,11... | collective-permute-start | bytes 1032200 | tf_op jit(solution)/shard_map/ppermute | solution.py:19
  112.4 6.8 %collective-permute-start.27 = (bf16[336,256]{1,0:T(8,128)(2,1)S(1)}, bf16[336,256]{1,0:T(8,128)(2,1)S(1)}, u32[]{:S(2)}, u32[]{:S(2)}) collective-permute-start(bf16[336,256]{1,0:T(8,128)(2,1)S(1)} %slice.20), channel_id=1, source_target_pairs={{0,8},{8,16},{16,24},{24,28},{28,20},{20,12},{12,4},{4,0},{1,9},{9... | collective-permute-start | bytes 516104 | tf_op jit(solution)/shard_map/ppermute | solution.py:52
  114.1 7.0 %collective-permute-start.34 = (bf16[336,512]{1,0:T(8,128)(2,1)S(1)}, bf16[336,512]{1,0:T(8,128)(2,1)S(1)}, u32[]{:S(2)}, u32[]{:S(2)}) collective-permute-start(bf16[336,512]{1,0:T(8,128)(2,1)S(1)} %collective-permute-done.23.refs_5_.refs_23_.refs_14_), channel_id=1, source_target_pairs={{0,1},{1,0},{2,3},{3,2},{4,5},{5,4},{6,7},{7,6},{8,9},{9,8},{10,11... | collective-permute-start | bytes 1032200 | tf_op jit(solution)/shard_map/ppermute | solution.py:19
  114.3 6.8 %collective-permute-start.35 = (bf16[336,512]{1,0:T(8,128)(2,1)S(1)}, bf16[336,512]{1,0:T(8,128)(2,1)S(1)}, u32[]{:S(2)}, u32[]{:S(2)}) collective-permute-start(bf16[336,512]{1,0:T(8,128)(2,1)S(1)} %collective-permute-done.24.refs_6_.refs_24_.refs_15_), channel_id=1, source_target_pairs={{0,1},{1,0},{2,3},{3,2},{4,5},{5,4},{6,7},{7,6},{8,9},{9,8},{10,11... | collective-permute-start | bytes 1032200 | tf_op jit(solution)/shard_map/ppermute | solution.py:19
  114.6 6.5 %collective-permute-start.28 = (bf16[336,256]{1,0:T(8,128)(2,1)S(1)}, bf16[336,256]{1,0:T(8,128)(2,1)S(1)}, u32[]{:S(2)}, u32[]{:S(2)}) collective-permute-start(bf16[336,256]{1,0:T(8,128)(2,1)S(1)} %slice.23), channel_id=1, source_target_pairs={{0,4},{8,0},{16,8},{24,16},{28,24},{20,28},{12,20},{4,12},{1,5},{9... | collective-permute-start | bytes 516104 | tf_op jit(solution)/shard_map/ppermute | solution.py:52
  119.3 1.9 %collective-permute-start.36 = (bf16[336,256]{1,0:T(8,128)(2,1)S(1)}, bf16[336,256]{1,0:T(8,128)(2,1)S(1)}, u32[]{:S(2)}, u32[]{:S(2)}) collective-permute-start(bf16[336,256]{1,0:T(8,128)(2,1)S(1)} %collective-permute-done.27.refs_7_.refs_25_.refs_16_), channel_id=1, source_target_pairs={{0,1},{1,0},{2,3},{3,2},{4,5},{5,4},{6,7},{7,6},{8,9},{9,8},{10,11... | collective-permute-start | bytes 516104 | tf_op jit(solution)/shard_map/ppermute | solution.py:19
  121.1 1.4 %collective-permute-start.37 = (bf16[336,256]{1,0:T(8,128)(2,1)S(1)}, bf16[336,256]{1,0:T(8,128)(2,1)S(1)}, u32[]{:S(2)}, u32[]{:S(2)}) collective-permute-start(bf16[336,256]{1,0:T(8,128)(2,1)S(1)} %collective-permute-done.28.refs_8_.refs_26_.refs_17_), channel_id=1, source_target_pairs={{0,1},{1,0},{2,3},{3,2},{4,5},{5,4},{6,7},{7,6},{8,9},{9,8},{10,11... | collective-permute-start | bytes 516104 | tf_op jit(solution)/shard_map/ppermute | solution.py:19
  123.2 9.3 %collective-permute-start.38 = (bf16[256,256]{1,0:T(8,128)(2,1)S(1)}, bf16[256,256]{1,0:T(8,128)(2,1)S(1)}, u32[]{:S(2)}, u32[]{:S(2)}) collective-permute-start(bf16[256,256]{1,0:T(8,128)(2,1)S(1)} %get-tuple-element.66.refs_0_), channel_id=1, source_target_pairs={{0,2},{1,3},{2,0},{3,1},{4,6},{5,7},{6,4},{7,5},{8,10},{9,11},{10,... | collective-permute-start | bytes 393224 | tf_op jit(solution)/shard_map/ppermute | solution.py:19
where the time goes:
time: 133 us
  waiting for transfers between devices  71.8 us (54%)
  starting transfers between devices  31.6 us (24%)
  Pallas kernels  25.5 us (19%)
  matrix products  1.55 us (1%)
    ppermute x16, waiting for transfers between devices, ring_step(): return lax.ppermute(block, 'wide', pairs)  51.4 us
    pallas_call x10, Pallas kernels, call(): pl.pallas_call(body, name=name, out_shape=outs, grid_spec=pltpu.PrefetchS...  25.5 us
    ppermute x23, waiting for transfers between devices, swap(): return lax.ppermute(block, 'narrow', [(n, n ^ bit) for n in range(size)])  20.4 us
    ppermute x16, starting transfers between devices, ring_step(): return lax.ppermute(block, 'wide', pairs)  17.9 us
    ppermute x23, starting transfers between devices, swap(): return lax.ppermute(block, 'narrow', [(n, n ^ bit) for n in range(size)])  13.7 us
  transfers between devices with their start and end apart: 39, of which 18 were waited for; matrix products, arithmetic and copies ran while one was open for 1% of the time, Pallas kernels for 13%

commit v1 on v0

--- a/solution.py
+++ b/solution.py
@@ -9,6 +9,7 @@
 
 HD = 128
 EPSILON = 1e-05
+EARLY = 3
 F32 = jnp.float32
 BF16 = jnp.bfloat16
 MIB = 1 << 20
@@ -52,17 +53,15 @@
     return lax.ppermute(block, "wide", pairs)
 
 
-def next_round(pair, *earlier):
-    up, down = (after(b, *earlier) for b in pair)
-    return ring_step(up, 1), ring_step(down, -1)
-
-
-def halves(pair, axis):
-    size = pair[0].shape[axis] // 2
-    return (
-        lax.slice_in_dim(pair[0], 0, size, axis=axis),
-        lax.slice_in_dim(pair[1], size, 2 * size, axis=axis),
-    )
+class Ring:
+    def __init__(self):
+        self.arrived = []
+
+    def step(self, *pair):
+        held = self.arrived[-2] if len(self.arrived) > 1 else ((), ())
+        up, down = (after(b, *h) for b, h in zip(pair, held))
+        self.arrived.append(((ring_step(up, 1),), (ring_step(down, -1),)))
+        return [self.arrived[-1][0][0], self.arrived[-1][1][0]]
 
 
 def dot(a, b):
@@ -96,35 +95,60 @@
                 add(j, dot(x_ref[...], w_ref[...]))
 
 
-def project_start(count, p_ref, *refs):
-    x_refs, w_refs, out = refs[:count], refs[count : count + 3], refs[-1]
-    cols = w_refs[0].shape[1]
-
-    @pl.when(pl.program_id(0) == 0)
-    def _():
-        out[...] = jnp.zeros_like(out)
-
-    def add(j, product):
-        out[:, j * cols : (j + 1) * cols] += product
-
-    add_products(x_refs, w_refs, add)
-
-
-def stage(ds, p_ref, *refs):
-    *refs, sems = refs
-    weights, caches, outs = refs[:3], refs[3:5], refs[5:]
-    rows = outs[0].shape[0]
+def row_of(values):
+    return jnp.transpose(jnp.broadcast_to(values, (values.shape[0], 128)))[:8]
+
+
+def embed(p_ref, latent_ref, actions_ref, table_ref, gain_ref, tokens_out, block_out):
+    count = latent_ref.shape[0]
+    shape = (table_ref.shape[0], count)
+    onehot = (lax.broadcasted_iota(jnp.int32, shape, 0) == actions_ref[...]).astype(BF16)
+    picked = lax.dot_general(
+        onehot, table_ref[...], (((0,), (0,)), ((), ())), preferred_element_type=F32
+    )
+    tokens = latent_ref[...].astype(F32) + picked
+    tokens_out[...] = tokens
+    block_out[:count] = (tokens * gain_ref[...]).astype(BF16)
+    block_out[count:] = jnp.zeros_like(block_out[count:])
+    rest = row_of(jnp.sum(tokens * tokens, axis=1, keepdims=True))[:1]
+    rows = lax.broadcasted_iota(jnp.int32, (16, count), 0)
+    terms = jnp.zeros((16, count), F32)
+    for k in range(3):
+        term = rest.astype(BF16).astype(F32)
+        terms = jnp.where(rows == k, term, terms)
+        rest = rest - term
+    block_out[count:, :count] = terms.astype(BF16)
+
+
+def begin(near, far, scenes, p_ref, *refs):
+    count = scenes * len(near)
+    x_refs, weights, caches = refs[:count], refs[count : count + 3], refs[count + 3 : count + 5]
+    acc, *outs, held, sems = refs[count + 5 :]
+    size, cols = held.shape[1:]
     copies = []
-    for i, d in enumerate(ds):
-        start = pl.multiple_of((p_ref[0] ^ d) * rows, rows)
-        copies += [(w.at[pl.ds(start, rows)], outs[i * 3 + j]) for j, w in enumerate(weights)]
-    copies += list(zip(caches, outs[-2:]))
-    copies = [
-        pltpu.make_async_copy(src, dst, sems.at[k]) for k, (src, dst) in enumerate(copies)
-    ]
-    for copy in copies:
-        copy.start()
-    for copy in copies:
+
+    def send(src, dst):
+        copies.append(pltpu.make_async_copy(src, dst, sems.at[len(copies)]))
+        copies[-1].start()
+
+    for i, d in enumerate(near + far):
+        start = pl.multiple_of((p_ref[0] ^ d) * size, size)
+        for j, w_ref in enumerate(weights):
+            k = i * 3 + j
+            send(
+                w_ref.at[pl.ds(start, size)],
+                held.at[k] if i < len(near) else outs[k - 3 * len(near)],
+            )
+    for src, dst in zip(caches, outs[-2:]):
+        send(src, dst)
+    for i in range(len(near)):
+        x = jnp.concatenate([ref[...] for ref in x_refs[i * scenes : (i + 1) * scenes]], axis=0)
+        for j in range(3):
+            copies[i * 3 + j].wait()
+            product = dot(x, held[i * 3 + j])
+            at = slice(j * cols, (j + 1) * cols)
+            acc[:, at] = product if i == 0 else acc[:, at] + product
+    for copy in copies[3 * len(near) :]:
         copy.wait()
 
 
@@ -139,17 +163,19 @@
         out[:, at] = total
 
 
-def attend(count, full_width, p_ref, acc_ref, squares_ref, keys_ref, values_ref, *refs):
+def attend(count, sources, full_width, p_ref, acc_ref, keys_ref, values_ref, *refs):
+    squares_refs, refs = refs[:sources], refs[sources:]
     project_more(count, p_ref, acc_ref, *refs[:-2], refs[-1])
     out, acc = refs[-2:]
     cols = refs[count].shape[1]
-    attend_heads(full_width, cols, squares_ref, keys_ref, values_ref, out, acc)
-
-
-def attend_heads(full_width, cols, squares_ref, keys_ref, values_ref, out, acc):
+    squares = sum(jnp.sum(ref[:8].astype(F32), axis=0, keepdims=True) for ref in squares_refs)
+    attend_heads(full_width, cols, squares, keys_ref, values_ref, out, acc)
+
+
+def attend_heads(full_width, cols, squares, keys_ref, values_ref, out, acc):
     scenes = keys_ref.shape[0]
     branch = acc.shape[0] // scenes
-    inverse = column(lax.rsqrt(squares_ref[:1] / full_width + EPSILON))
+    inverse = column(lax.rsqrt(squares / full_width + EPSILON))
     scaling = HD ** (-0.5)
     for s in range(scenes):
         rows = slice(s * branch, (s + 1) * branch)
@@ -181,26 +207,13 @@
             out[rows, at] = mixed.astype(BF16)
 
 
-def update_start(count, p_ref, tokens_ref, *refs):
-    x_refs, w_ref, out = refs[:count], refs[count], refs[-1]
+def update(count, p_ref, tokens_ref, gain_ref, policy_ref, value_ref, *refs):
+    x_refs, w_ref = refs[:count], refs[count]
+    latent_out, keep_out, give_out, squares_out, turned_out, acc = refs[-6:]
 
     @pl.when(pl.program_id(0) == 0)
     def _():
-        out[...] = tokens_ref[...]
-
-    def add(j, product):
-        out[...] += product
-
-    add_products(x_refs, [w_ref], add)
-
-
-def update_end(count, p_ref, acc_ref, gain_ref, policy_ref, value_ref, *refs):
-    x_refs, w_ref = refs[:count], refs[count]
-    latent_out, turned_out, squares_out, keep_out, give_out, acc = refs[count + 1 :]
-
-    @pl.when(pl.program_id(0) == 0)
-    def _():
-        acc[...] = acc_ref[...]
+        acc[...] = tokens_ref[...]
 
     def add(j, product):
         acc[...] += product
@@ -212,7 +225,7 @@
         state = acc[...]
         latent_out[...] = state.astype(BF16)
         squares = jnp.sum(state * state, axis=1, keepdims=True)
-        squares_out[...] = jnp.transpose(jnp.broadcast_to(squares, (squares.shape[0], 128)))[:8]
+        squares_out[...] = row_of(squares)
         gained = (state * gain_ref[...]).astype(BF16)
         turned_out[...] = jnp.transpose(gained)
         policy = dot(gained, policy_ref[...])
@@ -336,9 +349,7 @@
     turned_count, count = counts
     turned, own, other = refs[:turned_count], refs[turned_count:][:count], refs[turned_count:][count:-2]
     policy_out, value_out = refs[-2:]
-    upper = pl.program_id(0) < pl.num_programs(0) // 2
-    *turned, ahead, back = [ref[...] for ref in turned]
-    turned = jnp.concatenate([*turned, jnp.where(upper, ahead, back)], axis=1)
+    turned = jnp.concatenate([ref[...] for ref in turned], axis=1)
 
     def product(d_refs):
         *shards, ahead, back = [ref[...] for ref in d_refs]
@@ -356,12 +367,13 @@
         policy_out[...] = product(other)
 
 
-def call(body, name, place, steps, operands, in_specs, outs, out_specs, flops, limit, scratch=()):
+def call(body, name, place, steps, operands, in_specs, outs, out_specs, flops, limit, scratch=(), aliases=None):
     bytes_accessed = sum(x.size * x.dtype.itemsize for x in (*operands, *outs))
     return pl.pallas_call(
         body,
         name=name,
         out_shape=outs,
+        input_output_aliases=aliases or {},
         grid_spec=pltpu.PrefetchScalarGridSpec(
             num_scalar_prefetch=1,
             grid=(steps,),
@@ -413,102 +425,134 @@
     direct = list(range(2, narrow_size, 2))
     passed = [d + 1 for d in direct]
 
-    action_onehot = (
-        actions[:, None] == jnp.arange(action_count, dtype=jnp.int32)[None, :]
-    ).astype(BF16)
-    tokens = latent.astype(F32) + dot(action_onehot, action_table)
-    gained = (tokens * norm1_gain).astype(BF16)
-    squares = jnp.sum(tokens * tokens, axis=1)
-    squares = squares + swap(squares, 1)
-    blocks = far_blocks(gained)
-    blocks[1] = swap(gained, 1)
-
-    weights = [pltpu.with_memory_space_constraint(w, pltpu.HBM) for w in (w_query, w_key, w_value)]
-
-    def weight_specs(ds):
-        return [weight_spec(ds, width, cols)] * 3
-
+    far = direct + passed
+    scenes = key_cache.shape[0]
+    branch = rows // scenes
+    hbm = functools.partial(pltpu.with_memory_space_constraint, memory_space=pltpu.HBM)
+
+    tokens, blocks = [], []
+    block_shape = (branch + 16, width)
+    state_spec = whole((branch, width))
+    for s in range(scenes):
+        at = functools.partial(lambda s, i, p: (s, 0), s)
+        one_tokens, block = call(
+            embed, f"embed{s}", place, 1,
+            [hbm(latent), actions[None, :], hbm(action_table), norm1_gain[None, :]],
+            [
+                pl.BlockSpec((branch, width), at),
+                pl.BlockSpec((1, branch), functools.partial(lambda s, i, p: (0, s), s)),
+                whole(action_table.shape), whole((1, width)),
+            ],
+            [
+                jax.ShapeDtypeStruct((branch, width), F32),
+                jax.ShapeDtypeStruct(block_shape, BF16),
+            ],
+            [state_spec, whole(block_shape)], 2 * branch * width * action_count, 8 * MIB,
+        )
+        tokens.append(one_tokens)
+        blocks.append({**far_blocks(block), 1: swap(block, 1)})
+
+    weights = [hbm(w) for w in (w_query, w_key, w_value)]
+    x_spec = whole((branch, width))
     acc_shape = jax.ShapeDtypeStruct((rows, 3 * cols), F32)
-    acc_spec = whole((rows, 3 * cols))
-    x_spec = whole((rows, width))
-    flops = 2 * rows * width * 3 * cols
-    acc = call(
-        functools.partial(project_start, len(near)), "project_near", place, len(near),
-        [*(blocks[d] for d in near), *weights],
-        [*[x_spec] * len(near), *weight_specs(near)],
-        [acc_shape], [acc_spec], flops * len(near), 20 * MIB,
-    )[0]
-    far = direct + passed
-    block_shape = jax.ShapeDtypeStruct((width, cols), BF16)
+    weight_shape = jax.ShapeDtypeStruct((width, cols), BF16)
+    weight_block = whole((width, cols))
     cache_shape = jax.ShapeDtypeStruct(key_cache.shape, BF16)
-    outs = [block_shape] * (3 * len(far)) + [cache_shape] * 2
+    outs = [weight_shape] * (3 * len(far)) + [cache_shape] * 2
     anywhere = pl.BlockSpec(memory_space=pl.ANY)
-    *staged, keys, values = call(
-        functools.partial(stage, far), "stage", place, 1,
-        [*weights, *(pltpu.with_memory_space_constraint(c, pltpu.HBM) for c in (key_cache, value_cache))],
-        [anywhere] * 5, outs, [anywhere] * len(outs),
-        0, 4 * MIB, [pltpu.SemaphoreType.DMA((len(outs),))],
+    flops = 2 * branch * width * 3 * cols
+    acc, *staged, keys, values = call(
+        functools.partial(begin, near, far, scenes), "begin", place, 1,
+        [
+            *(blocks[s][d] for d in near for s in range(scenes)), *weights,
+            hbm(key_cache), hbm(value_cache),
+        ],
+        [*[x_spec] * (scenes * len(near)), *[anywhere] * 5],
+        [acc_shape, *outs], [whole(acc_shape.shape), *[anywhere] * len(outs)],
+        flops * scenes * len(near), 20 * MIB,
+        [
+            pltpu.VMEM((3 * len(near), width, cols), BF16),
+            pltpu.SemaphoreType.DMA((3 * len(near) + len(outs),)),
+        ],
     )
     staged_direct = staged[: 3 * len(direct)]
     staged_passed = staged[3 * len(direct) :]
-    block_spec = whole((width, cols))
-    blocks = pass_blocks(blocks, acc, *staged, keys, values)
-    for bit in far_bits():
-        squares = squares + swap(after(squares, acc), bit)
-    squares = jnp.broadcast_to(squares[None, :], (8, rows))
-    acc = call(
-        functools.partial(project_more, len(direct)), "project_direct", place, 1,
-        [acc, *(blocks[d] for d in direct), *staged_direct],
-        [acc_spec, *[x_spec] * len(direct), *[block_spec] * len(staged_direct)],
-        [acc_shape], [acc_spec], flops * len(direct), 24 * MIB,
-    )[0]
-    cache_spec = whole(key_cache.shape)
-    attended = call(
-        functools.partial(attend, len(passed), full_width), "attend", place, 1,
-        [acc, squares, keys, values, *(blocks[d] for d in passed), *staged_passed],
-        [
-            acc_spec, whole(squares.shape), cache_spec, cache_spec,
-            *[x_spec] * len(passed), *[block_spec] * len(staged_passed),
-        ],
-        [jax.ShapeDtypeStruct((rows, cols), BF16)], [whole((rows, cols))],
-        flops * len(passed), 32 * MIB, [pltpu.VMEM((rows, 3 * cols), F32)],
-    )[0]
-
-    blocks = far_blocks(attended)
-    blocks[1] = swap(attended, 1)
-    x_spec = whole((rows, cols))
-    state_spec = whole((rows, width))
-    state_shape = jax.ShapeDtypeStruct((rows, width), F32)
-    flops = 2 * rows * width * cols
-    acc = call(
-        functools.partial(update_start, len(near)), "update_near", place, len(near),
-        [tokens, *(blocks[d] for d in near), w_out],
-        [state_spec, *[x_spec] * len(near), weight_spec(near, cols, width)],
-        [state_shape], [state_spec], flops * len(near), 16 * MIB,
-    )[0]
-    blocks = pass_blocks(blocks, acc)
+
+    part_spec = whole((branch, 3 * cols))
+    squares_spec = pl.BlockSpec((16, branch), lambda i, p: (branch // 16, 0))
+    attended = []
+    for s in range(scenes):
+        blocks[s] = pass_blocks(blocks[s], acc)
+        part = call(
+            functools.partial(project_more, len(direct)), f"project{s}", place, 1,
+            [acc, *(blocks[s][d] for d in direct), *staged_direct],
+            [
+                pl.BlockSpec(
+                    (branch, 3 * cols), functools.partial(lambda s, i, p: (s, 0), s)
+                ),
+                *[x_spec] * len(direct), *[weight_block] * len(staged_direct),
+            ],
+            [jax.ShapeDtypeStruct((branch, 3 * cols), F32)], [part_spec],
+            flops * len(direct), 20 * MIB,
+        )[0]
+        cache_spec = pl.BlockSpec(
+            (1, *key_cache.shape[1:]), functools.partial(lambda s, i, p: (s, 0, 0), s)
+        )
+        one = call(
+            functools.partial(attend, len(passed), narrow_size, full_width), f"attend{s}", place, 1,
+            [
+                part, keys, values, *blocks[s].values(),
+                *(blocks[s][d] for d in passed), *staged_passed,
+            ],
+            [
+                part_spec, cache_spec, cache_spec, *[squares_spec] * narrow_size,
+                *[x_spec] * len(passed), *[weight_block] * len(staged_passed),
+            ],
+            [jax.ShapeDtypeStruct((branch, cols), BF16)], [whole((branch, cols))],
+            flops * len(passed), 20 * MIB, [pltpu.VMEM((branch, 3 * cols), F32)],
+        )[0]
+        attended.append({**far_blocks(one), 1: swap(one, 1)})
+
     half = (rows, hidden_count)
-    new_latent, turned, squares, keep, give = call(
-        functools.partial(update_end, len(far)), "update_end", place, len(far),
-        [acc, norm2_gain[None, :], policy_in, value_in, *(blocks[d] for d in far), w_out],
-        [
-            state_spec, whole((1, width)), whole(policy_in.shape), whole(value_in.shape),
-            *[x_spec] * len(far), weight_spec(far, cols, width),
-        ],
-        [
-            jax.ShapeDtypeStruct((rows, width), BF16),
-            jax.ShapeDtypeStruct((width, rows), BF16),
-            jax.ShapeDtypeStruct((8, rows), F32),
-            jax.ShapeDtypeStruct(half, F32),
-            jax.ShapeDtypeStruct(half, BF16),
-        ],
-        [state_spec, whole((width, rows)), whole((8, rows)), whole(half), whole(half)],
-        flops * len(far) + 4 * rows * width * hidden_count, 32 * MIB,
-        [pltpu.VMEM((rows, width), F32)],
-    )
-    rounds = wide_size // 2
-    turned_rounds = [(turned, turned)]
-    turned_rounds.append(next_round(turned_rounds[0]))
+    full_shapes = [
+        jax.ShapeDtypeStruct((rows, width), BF16),
+        jax.ShapeDtypeStruct(half, F32),
+        jax.ShapeDtypeStruct(half, BF16),
+        jax.ShapeDtypeStruct((8, rows), F32),
+    ]
+    filled, turned, shards = [], [], []
+    ring = Ring()
+    for s in range(scenes):
+        ds = near + far
+        around = pass_blocks(attended[s])
+        at = functools.partial(lambda s, i, p: (s, 0), s)
+        operands = [
+            tokens[s], norm2_gain[None, :], policy_in, value_in,
+            *(around[d] for d in ds), w_out, *filled,
+        ]
+        *filled, one = call(
+            functools.partial(update, len(ds)), f"update{s}", place, len(ds), operands,
+            [
+                state_spec, whole((1, width)), whole(policy_in.shape), whole(value_in.shape),
+                *[whole((branch, cols))] * len(ds), weight_spec(ds, cols, width),
+                *[anywhere] * len(filled),
+            ],
+            [*full_shapes, jax.ShapeDtypeStruct((width, branch), BF16)],
+            [
+                pl.BlockSpec((branch, width), at),
+                pl.BlockSpec((branch, hidden_count), at),
+                pl.BlockSpec((branch, hidden_count), at),
+                pl.BlockSpec((8, branch), functools.partial(lambda s, i, p: (0, s), s)),
+                whole((width, branch)),
+            ],
+            2 * branch * width * (cols * len(ds) + 2 * hidden_count), 28 * MIB,
+            [pltpu.VMEM((branch, width), F32)],
+            {1 + len(operands) - len(filled) + k: k for k in range(len(filled))},
+        )
+        turned.append(one)
+        if s == 0:
+            shards.append([ring.step(one, one)])
+    new_latent, keep, give, squares = filled
 
     for bit in (1, *far_bits()):
         squares = squares + swap(squares, bit)
@@ -517,7 +561,10 @@
     *upper, last = far_bits()
     for bit in upper:
         mine = (mine.astype(F32) + swap(mine, bit).astype(F32)).astype(BF16)
-    theirs = after(swap(mine, last), *turned_rounds[1])
+    rounds = wide_size // 2
+    while len(shards[0]) < min(EARLY, rounds - 1):
+        shards[0].append(ring.step(*shards[0][-1]))
+    theirs = after(swap(mine, last), *shards[0][-1])
     quarter = hidden_count // chips // 4
     payload_shape = (rows + quarter + 16, hidden_count)
     payload, give = call(
@@ -540,15 +587,27 @@
     taken = jnp.where(first, payload[rows : rows + quarter], swap(give, 1))
     payload = lax.dynamic_update_slice(payload, taken, (rows, 0))
 
-    payload_rounds = [(payload, payload)]
-    for step in range(1, rounds + 1):
-        if step < rounds:
-            ahead = turned_rounds[step] if step < rounds - 1 else halves(turned_rounds[step], 0)
-            turned_rounds.append(next_round(ahead))
-        ahead = payload_rounds[step - 1]
-        ahead = ahead if step < rounds else halves(ahead, 1)
-        payload_rounds.append(next_round(ahead, *turned_rounds[step]))
-    turned_all = [turned, *(b for pair in turned_rounds[1:] for b in pair)]
+    shards += [[ring.step(one, one)] for one in turned[1:]]
+    payload_rounds = [[payload, payload]]
+    for shard in shards:
+        while len(shard) < rounds - 1:
+            if len(payload_rounds) < rounds:
+                payload_rounds.append(ring.step(*payload_rounds[-1]))
+            shard.append(ring.step(*shard[-1]))
+    while len(payload_rounds) < rounds:
+        payload_rounds.append(ring.step(*payload_rounds[-1]))
+    cut = scenes // 2
+    for one, other in zip(shards[:cut], shards[cut:]):
+        up, down = ring.step(one[-1][0], other[-1][1])
+        one.append([up])
+        other.append([down])
+    size = hidden_count // 2
+    up, down = payload_rounds[-1]
+    payload_rounds.append(ring.step(up[:, :size], down[:, size:]))
+    turned_all = list(turned)
+    for step in range(rounds):
+        for way in range(len(shards[0][step])):
+            turned_all += [shard[step][way] for shard in shards]
     payload_own = [payload, *(b for pair in payload_rounds[1:] for b in pair)]
     payload_other = [swap(b, 1) for b in payload_own]
 
@@ -579,12 +638,7 @@
     )[0]
 
     block = 256
-    half_steps = width // block // 2
-    turned_specs = [pl.BlockSpec((block, rows), lambda i, p: (i, 0))] * (len(turned_all) - 2)
-    turned_specs += [
-        pl.BlockSpec((block, rows), lambda i, p: (jnp.minimum(i, half_steps - 1), 0)),
-        pl.BlockSpec((block, rows), lambda i, p: (jnp.maximum(i - half_steps, 0), 0)),
-    ]
+    turned_specs = [pl.BlockSpec((block, branch), lambda i, p: (i, 0))] * len(turned_all)
     dpre_specs = [
         pl.BlockSpec((rows, b.shape[1]), lambda i, p: (0, 0), pipeline_mode=pl.Buffered(1))
         for b in payload_own

time: 133 us -> 130 us (0.977)
  waiting for transfers between devices: 71.8 us -> 68.7 us
  Pallas kernels: 25.5 us -> 27.3 us
  matrix products: 1.55 us -> 0 us
    ppermute x23 -> x27, starting transfers between devices: 13.7 us -> 8.71 us  [swap(): return lax.ppermute(block, 'narrow', [(n, n ^ bit) for n in range(size)])]
    ppermute x16 -> x22, starting transfers between devices: 17.9 us -> 22.4 us  [ring_step(): return lax.ppermute(block, 'wide', pairs)]
    ppermute x16 -> x22, waiting for transfers between devices: 51.4 us -> 48.8 us  [ring_step(): return lax.ppermute(block, 'wide', pairs)]
    pallas_call x10 -> x13, Pallas kernels: 25.5 us -> 27.3 us  [call(): pl.pallas_call(body, name=name, out_shape=outs, input_output_aliases=alia...]
    dot_general x1 -> x0, matrix products: 1.55 us -> none  [dot(): return jnp.dot(a, b, preferred_element_type=F32)]
    ppermute x23 -> x27, waiting for transfers between devices: 20.4 us -> 19.9 us  [swap(): return lax.ppermute(block, 'narrow', [(n, n ^ bit) for n in range(size)])]
  transfers between devices with their start and end apart: 39 -> 49, of which waited for: 18 -> 25; matrix products, arithmetic and copies ran while one was open for 1% -> 1% of each run, Pallas kernels for 13% -> 18%
where the time goes in v1:
time: 130 us
  waiting for transfers between devices  68.7 us (53%)
  starting transfers between devices  31.2 us (24%)
  Pallas kernels  27.3 us (21%)
  local copies, waits for them, and re-layouts  1.43 us (1%)
    ppermute x22, waiting for transfers between devices, ring_step(): return lax.ppermute(block, 'wide', pairs)  48.8 us
    pallas_call x13, Pallas kernels, call(): pl.pallas_call(body, name=name, out_shape=outs, input_output_aliases=alia...  27.3 us
    ppermute x22, starting transfers between devices, ring_step(): return lax.ppermute(block, 'wide', pairs)  22.4 us
    ppermute x27, waiting for transfers between devices, swap(): return lax.ppermute(block, 'narrow', [(n, n ^ bit) for n in range(size)])  19.9 us
    ppermute x27, starting transfers between devices, swap(): return lax.ppermute(block, 'narrow', [(n, n ^ bit) for n in range(size)])  8.71 us
  transfers between devices with their start and end apart: 49, of which 25 were waited for; matrix products, arithmetic and copies ran while one was open for 1% of the time, Pallas kernels for 18%

profile of v1, /device:TPU:0, one launch (start us, length us, event | category | flops | bytes accessed | tf_op | source)
XLA Modules:
  0.0 130.2 jit_solution(8448133992601604907)
XLA Ops:
  0.6 0.7 copy-done.5
  1.3 0.7 copy-done.6
  2.0 1.5 %embed0.1 = (f32[128,1024]{1,0:T(8,128)S(1)}, bf16[144,1024]{1,0:T(8,128)(2,1)S(1)}) custom-call(s32[1]{0:T(128)} %bitcast.p_ref, bf16[256,1024]{1,0:T(8,128)(2,1)} %latent_ref.3, s32[1,256]{1,0:T(1,128)S(1)} %bitcast.11, bf16[256,1024]{1,0:T(8,128)(2,1)} %table_ref.3, f32[1,1024]{1,0:T(1,128)S(1)} %bitcast.9), custom_call_target="tpu_custom_call" | custom-call | flops 67108864 | bytes 1872896 | tf_op jit(solution)/shard_map/embed0/pallas_call | solution.py:372
  3.5 0.5 collective-permute-start
  4.0 1.5 %embed1.1 = (f32[128,1024]{1,0:T(8,128)S(1)}, bf16[144,1024]{1,0:T(8,128)(2,1)S(1)}) custom-call(s32[1]{0:T(128)} %bitcast.p_ref, bf16[256,1024]{1,0:T(8,128)(2,1)} %latent_ref.3, s32[1,256]{1,0:T(1,128)S(1)} %bitcast.12, bf16[256,1024]{1,0:T(8,128)(2,1)} %table_ref.3, f32[1,1024]{1,0:T(1,128)S(1)} %bitcast.10), custom_call_target="tpu_custom_call" | custom-call | flops 67108864 | bytes 1872896 | tf_op jit(solution)/shard_map/embed1/pallas_call | solution.py:372
  5.6 3.0 %collective-permute-start.7 = (bf16[144,1024]{1,0:T(8,128)(2,1)S(1)}, bf16[144,1024]{1,0:T(8,128)(2,1)S(1)}, u32[]{:S(2)}, u32[]{:S(2)}) collective-permute-start(bf16[144,1024]{1,0:T(8,128)(2,1)S(1)} %get-tuple-element.58.refs_0_), channel_id=1, source_target_pairs={{0,2},{1,3},{2,0},{3,1},{4,6},{5,7},{6,4},{7,5},{8,10},{9,11},{10,... | collective-permute-start | bytes 884744 | tf_op jit(solution)/shard_map/ppermute | solution.py:20
  8.6 5.3 %begin.1 = (f32[256,1536]{1,0:T(8,128)S(1)}, bf16[1024,512]{1,0:T(8,128)(2,1)S(1)}, bf16[1024,512]{1,0:T(8,128)(2,1)S(1)}, bf16[1024,512]{1,0:T(8,128)(2,1)S(1)}...) custom-call(s32[1]{0:T(128)} %bitcast.p_ref, ...), custom_call_target="tpu_custom_call" | custom-call | flops 1610612736 | bytes 25821184 | tf_op jit(solution)/shard_map/begin/pallas_call | solution.py:372
  14.0 2.4 %collective-permute-done.7.refs_0_.refs_1_ = bf16[144,1024]{1,0:T(8,128)(2,1)S(1)} collective-permute-done((bf16[144,1024]{1,0:T(8,128)(2,1)S(1)}, bf16[144,1024]{1,0:T(8,128)(2,1)S(1)}, u32[]{:S(2)}, u32[]{:S(2)}) %collective-permute-start.7) | collective-permute-done | bytes 294944 | tf_op jit(solution)/shard_map/ppermute | solution.py:20
  16.4 5.8 %collective-permute-done.2.refs_0_.refs_1_ = bf16[144,1024]{1,0:T(8,128)(2,1)S(1)} collective-permute-done((bf16[144,1024]{1,0:T(8,128)(2,1)S(1)}, bf16[144,1024]{1,0:T(8,128)(2,1)S(1)}, u32[]{:S(2)}, u32[]{:S(2)}) %collective-permute-start.2) | collective-permute-done | bytes 294944 | tf_op jit(solution)/shard_map/ppermute | solution.py:20
  22.2 0.6 project0.1.acc_ref
  22.8 2.0 %attend0.1.refs_0_ = bf16[128,512]{1,0:T(8,128)(2,1)S(1)} custom-call(s32[1]{0:T(128)} %bitcast.p_ref, f32[128,1536]{1,0:T(8,128)S(1)} %project0.1.acc_ref, bf16[2,512,512]{2,1,0:T(8,128)(2,1)S(1)} %get-tuple-element.64.keys_ref, bf16[2,512,512]{2,1,0:T(8,128)(2,1)S(1)} %get-tuple-element.65.values_ref, bf16[144,1024]{1,0:T(8,128)(2,1)S(1)} %get-tuple-element.58.refs_0_, ...), custom_call_target="tpu_custom_call" | custom-call | flops 402653184 | bytes 7634944 | tf_op jit(solution)/shard_map/attend0/pallas_call | solution.py:372
  24.8 1.8 %collective-permute-start.10 = (bf16[128,512]{1,0:T(8,128)(2,1)S(1)}, bf16[128,512]{1,0:T(8,128)(2,1)S(1)}, u32[]{:S(2)}, u32[]{:S(2)}) collective-permute-start(bf16[128,512]{1,0:T(8,128)(2,1)S(1)} %attend0.1.refs_0_), channel_id=1, source_target_pairs={{0,2},{1,3},{2,0},{3,1},{4,6},{5,7},{6,4},{7,5},{8,10},{9,11},{10,... | collective-permute-start | bytes 393224 | tf_op jit(solution)/shard_map/ppermute | solution.py:20
  26.6 0.6 project1.1.acc_ref
  27.3 2.0 %attend1.1.refs_0_ = bf16[128,512]{1,0:T(8,128)(2,1)S(1)} custom-call(s32[1]{0:T(128)} %bitcast.p_ref, f32[128,1536]{1,0:T(8,128)S(1)} %project1.1.acc_ref, bf16[2,512,512]{2,1,0:T(8,128)(2,1)S(1)} %get-tuple-element.64.keys_ref, bf16[2,512,512]{2,1,0:T(8,128)(2,1)S(1)} %get-tuple-element.65.values_ref, ...), custom_call_target="tpu_custom_call" | custom-call | flops 402653184 | bytes 7634944 | tf_op jit(solution)/shard_map/attend1/pallas_call | solution.py:372
  29.7 1.1 collective-permute-done.10.refs_2_
  30.8 0.5 collective-permute-start.4
  31.3 3.7 %collective-permute-done.5.refs_2_ = bf16[128,512]{1,0:T(8,128)(2,1)S(1)} collective-permute-done((bf16[128,512]{1,0:T(8,128)(2,1)S(1)}, bf16[128,512]{1,0:T(8,128)(2,1)S(1)}, u32[]{:S(2)}, u32[]{:S(2)}) %collective-permute-start.5) | collective-permute-done | bytes 131104 | tf_op jit(solution)/shard_map/ppermute | solution.py:20
  35.0 2.4 %update0.1 = (bf16[256,1024]{1,0:T(8,128)(2,1)}, f32[256,512]{1,0:T(8,128)S(1)}, bf16[256,512]{1,0:T(8,128)(2,1)S(1)}, f32[8,256]{1,0:T(8,128)S(1)}, bf16[1024,128]{1,0:T(8,128)(2,1)S(1)}) custom-call(s32[1]{0:T(128)} %bitcast.p_ref, f32[128,1024]{1,0:T(8,128)S(1)} %get-tuple-element.70.tokens_ref, f32[1,1024]{1,0:T(1,128)S(1)} %bitcast.7, ...), custom_call_target="tpu_custom_call" | custom-call | flops 805306368 | bytes 8925184 | tf_op jit(solution)/shard_map/update0/pallas_call | solution.py:372
  37.5 1.6 %collective-permute-start.14 = (bf16[1024,128]{1,0:T(8,128)(2,1)S(1)}, bf16[1024,128]{1,0:T(8,128)(2,1)S(1)}, u32[]{:S(2)}, u32[]{:S(2)}) collective-permute-start(bf16[1024,128]{1,0:T(8,128)(2,1)S(1)} %get-tuple-element.79.refs_0_), channel_id=1, source_target_pairs={{0,8},{8,16},{16,24},{24,28},{28,20},{20,12},{12,4},{4,0},{1,9},{9... | collective-permute-start | bytes 786440 | tf_op jit(solution)/shard_map/ppermute | solution.py:53
  39.1 0.5 collective-permute-start.17
  39.6 2.5 %update1.1 = (bf16[256,1024]{1,0:T(8,128)(2,1)}, f32[256,512]{1,0:T(8,128)S(1)}, bf16[256,512]{1,0:T(8,128)(2,1)S(1)}, f32[8,256]{1,0:T(8,128)S(1)}, bf16[1024,128]{1,0:T(8,128)(2,1)S(1)}) custom-call(s32[1]{0:T(128)} %bitcast.p_ref, ...), custom_call_target="tpu_custom_call", output_to_operand_aliasing={{0}: (10, {}), {1}: (11, {}), {2}: (12, {}), {3}: (13, {})} | custom-call | flops 805306368 | bytes 10244096 | tf_op jit(solution)/shard_map/update1/pallas_call | solution.py:372
  42.0 4.2 %collective-permute-done.14.refs_2_ = bf16[1024,128]{1,0:T(8,128)(2,1)S(1)} collective-permute-done((bf16[1024,128]{1,0:T(8,128)(2,1)S(1)}, bf16[1024,128]{1,0:T(8,128)(2,1)S(1)}, u32[]{:S(2)}, u32[]{:S(2)}) %collective-permute-start.14) | collective-permute-done | bytes 262176 | tf_op jit(solution)/shard_map/ppermute | solution.py:53
  46.2 1.6 %collective-permute-start.15 = (bf16[1024,128]{1,0:T(8,128)(2,1)S(1)}, bf16[1024,128]{1,0:T(8,128)(2,1)S(1)}, u32[]{:S(2)}, u32[]{:S(2)}) collective-permute-start(bf16[1024,128]{1,0:T(8,128)(2,1)S(1)} %collective-permute-done.14.refs_2_), channel_id=1, source_target_pairs={{0,8},{8,16},{16,24},{24,28},{28,20},{20,12},{12,4},{4,0},{1,9},{9... | collective-permute-start | bytes 786440 | tf_op jit(solution)/shard_map/ppermute | solution.py:53
  47.8 0.5 collective-permute-start.18
  48.7 5.4 %collective-permute-done.15.refs_6_ = bf16[1024,128]{1,0:T(8,128)(2,1)S(1)} collective-permute-done((bf16[1024,128]{1,0:T(8,128)(2,1)S(1)}, bf16[1024,128]{1,0:T(8,128)(2,1)S(1)}, u32[]{:S(2)}, u32[]{:S(2)}) %collective-permute-start.15) | collective-permute-done | bytes 262176 | tf_op jit(solution)/shard_map/ppermute | solution.py:53
  54.1 1.6 %collective-permute-start.16 = (bf16[1024,128]{1,0:T(8,128)(2,1)S(1)}, bf16[1024,128]{1,0:T(8,128)(2,1)S(1)}, u32[]{:S(2)}, u32[]{:S(2)}) collective-permute-start(bf16[1024,128]{1,0:T(8,128)(2,1)S(1)} %collective-permute-done.15.refs_6_), channel_id=1, source_target_pairs={{0,8},{8,16},{16,24},{24,28},{28,20},{20,12},{12,4},{4,0},{1,9},{9... | collective-permute-start | bytes 786440 | tf_op jit(solution)/shard_map/ppermute | solution.py:53
  55.7 0.5 collective-permute-start.19
  56.2 1.2 collective-permute-done.20
  57.7 3.3 %collective-permute-done.21 = f32[8,256]{1,0:T(8,128)S(1)} collective-permute-done((f32[8,256]{1,0:T(8,128)S(1)}, f32[8,256]{1,0:T(8,128)S(1)}, u32[]{:S(2)}, u32[]{:S(2)}) %collective-permute-start.21) | collective-permute-done | bytes 8224 | tf_op jit(solution)/shard_map/ppermute | solution.py:20
  61.2 1.3 collective-permute-done.19.refs_12_
  62.5 1.1 heads.1
  63.7 1.2 collective-permute-done.22
  65.0 1.6 %collective-permute-start.23 = (bf16[336,512]{1,0:T(8,128)(2,1)S(1)}, bf16[336,512]{1,0:T(8,128)(2,1)S(1)}, u32[]{:S(2)}, u32[]{:S(2)}) collective-permute-start(bf16[336,512]{1,0:T(8,128)(2,1)S(1)} %select_dynamic-update-slice_fusion.refs_0_.refs_18_.refs_16_), channel_id=1, source_target_pairs={{0,8},{8,16},{16,24},{24,28},{28,20},{20,12},{12,4},{4,0},{1,9},{9... | collective-permute-start | bytes 1032200 | tf_op jit(solution)/shard_map/ppermute | solution.py:53
  67.0 1.6 %collective-permute-start.40 = (bf16[1024,128]{1,0:T(8,128)(2,1)S(1)}, bf16[1024,128]{1,0:T(8,128)(2,1)S(1)}, u32[]{:S(2)}, u32[]{:S(2)}) collective-permute-start(bf16[1024,128]{1,0:T(8,128)(2,1)S(1)} %get-tuple-element.97.refs_1_), channel_id=1, source_target_pairs={{0,8},{8,16},{16,24},{24,28},{28,20},{20,12},{12,4},{4,0},{1,9},{9... | collective-permute-start | bytes 786440 | tf_op jit(solution)/shard_map/ppermute | solution.py:53
  69.1 6.9 %collective-permute-done.23.refs_1_.refs_19_.refs_17_ = bf16[336,512]{1,0:T(8,128)(2,1)S(1)} collective-permute-done((bf16[336,512]{1,0:T(8,128)(2,1)S(1)}, bf16[336,512]{1,0:T(8,128)(2,1)S(1)}, u32[]{:S(2)}, u32[]{:S(2)}) %collective-permute-start.23) | collective-permute-done | bytes 344096 | tf_op jit(solution)/shard_map/ppermute | solution.py:53
  75.9 1.6 %collective-permute-start.25 = (bf16[336,512]{1,0:T(8,128)(2,1)S(1)}, bf16[336,512]{1,0:T(8,128)(2,1)S(1)}, u32[]{:S(2)}, u32[]{:S(2)}) collective-permute-start(bf16[336,512]{1,0:T(8,128)(2,1)S(1)} %collective-permute-done.23.refs_1_.refs_19_.refs_17_), channel_id=1, source_target_pairs={{0,8},{8,16},{16,24},{24,28},{28,20},{20,12},{12,4},{4,0},{1,9},{9... | collective-permute-start | bytes 1032200 | tf_op jit(solution)/shard_map/ppermute | solution.py:53
  77.5 4.0 %collective-permute-done.40.refs_3_ = bf16[1024,128]{1,0:T(8,128)(2,1)S(1)} collective-permute-done((bf16[1024,128]{1,0:T(8,128)(2,1)S(1)}, bf16[1024,128]{1,0:T(8,128)(2,1)S(1)}, u32[]{:S(2)}, u32[]{:S(2)}) %collective-permute-start.40) | collective-permute-done | bytes 262176 | tf_op jit(solution)/shard_map/ppermute | solution.py:53
  81.5 1.6 %collective-permute-start.42 = (bf16[1024,128]{1,0:T(8,128)(2,1)S(1)}, bf16[1024,128]{1,0:T(8,128)(2,1)S(1)}, u32[]{:S(2)}, u32[]{:S(2)}) collective-permute-start(bf16[1024,128]{1,0:T(8,128)(2,1)S(1)} %collective-permute-done.40.refs_3_), channel_id=1, source_target_pairs={{0,8},{8,16},{16,24},{24,28},{28,20},{20,12},{12,4},{4,0},{1,9},{9... | collective-permute-start | bytes 786440 | tf_op jit(solution)/shard_map/ppermute | solution.py:53
  83.6 0.5 collective-permute-start.26
  84.0 9.7 %collective-permute-done.42.refs_7_ = bf16[1024,128]{1,0:T(8,128)(2,1)S(1)} collective-permute-done((bf16[1024,128]{1,0:T(8,128)(2,1)S(1)}, bf16[1024,128]{1,0:T(8,128)(2,1)S(1)}, u32[]{:S(2)}, u32[]{:S(2)}) %collective-permute-start.42) | collective-permute-done | bytes 262176 | tf_op jit(solution)/shard_map/ppermute | solution.py:53
  93.8 1.6 %collective-permute-start.44 = (bf16[1024,128]{1,0:T(8,128)(2,1)S(1)}, bf16[1024,128]{1,0:T(8,128)(2,1)S(1)}, u32[]{:S(2)}, u32[]{:S(2)}) collective-permute-start(bf16[1024,128]{1,0:T(8,128)(2,1)S(1)} %collective-permute-done.42.refs_7_), channel_id=1, source_target_pairs={{0,8},{8,16},{16,24},{24,28},{28,20},{20,12},{12,4},{4,0},{1,9},{9... | collective-permute-start | bytes 786440 | tf_op jit(solution)/shard_map/ppermute | solution.py:53
  95.8 1.2 collective-permute-done.26.refs_4_.refs_22_.refs_20_
  97.0 1.6 %collective-permute-start.27 = (bf16[336,512]{1,0:T(8,128)(2,1)S(1)}, bf16[336,512]{1,0:T(8,128)(2,1)S(1)}, u32[]{:S(2)}, u32[]{:S(2)}) collective-permute-start(bf16[336,512]{1,0:T(8,128)(2,1)S(1)} %collective-permute-done.25.refs_3_.refs_21_.refs_19_), channel_id=1, source_target_pairs={{0,8},{8,16},{16,24},{24,28},{28,20},{20,12},{12,4},{4,0},{1,9},{9... | collective-permute-start | bytes 1032200 | tf_op jit(solution)/shard_map/ppermute | solution.py:53
  98.5 0.5 collective-permute-start.28
  99.0 4.0 %collective-permute-done.44.refs_11_ = bf16[1024,128]{1,0:T(8,128)(2,1)S(1)} collective-permute-done((bf16[1024,128]{1,0:T(8,128)(2,1)S(1)}, bf16[1024,128]{1,0:T(8,128)(2,1)S(1)}, u32[]{:S(2)}, u32[]{:S(2)}) %collective-permute-start.44) | collective-permute-done | bytes 262176 | tf_op jit(solution)/shard_map/ppermute | solution.py:53
  103.0 1.6 %collective-permute-done.45.refs_13_ = bf16[1024,128]{1,0:T(8,128)(2,1)S(1)} collective-permute-done((bf16[1024,128]{1,0:T(8,128)(2,1)S(1)}, bf16[1024,128]{1,0:T(8,128)(2,1)S(1)}, u32[]{:S(2)}, u32[]{:S(2)}) %collective-permute-start.45) | collective-permute-done | bytes 262176 | tf_op jit(solution)/shard_map/ppermute | solution.py:53
  104.6 0.5 collective-permute-start.35
  105.1 3.6 %collective-permute-done.27.refs_5_.refs_23_.refs_21_ = bf16[336,512]{1,0:T(8,128)(2,1)S(1)} collective-permute-done((bf16[336,512]{1,0:T(8,128)(2,1)S(1)}, bf16[336,512]{1,0:T(8,128)(2,1)S(1)}, u32[]{:S(2)}, u32[]{:S(2)}) %collective-permute-start.27) | collective-permute-done | bytes 344096 | tf_op jit(solution)/shard_map/ppermute | solution.py:53
  108.7 1.3 collective-permute-done.28.refs_6_.refs_24_.refs_22_
  110.0 1.6 %collective-permute-start.29 = (bf16[336,256]{1,0:T(8,128)(2,1)S(1)}, bf16[336,256]{1,0:T(8,128)(2,1)S(1)}, u32[]{:S(2)}, u32[]{:S(2)}) collective-permute-start(bf16[336,256]{1,0:T(8,128)(2,1)S(1)} %slice.12), channel_id=1, source_target_pairs={{0,8},{8,16},{16,24},{24,28},{28,20},{20,12},{12,4},{4,0},{1,9},{9... | collective-permute-start | bytes 516104 | tf_op jit(solution)/shard_map/ppermute | solution.py:53
  111.6 0.5 collective-permute-start.30
  112.1 1.6 %collective-permute-start.46 = (bf16[1024,128]{1,0:T(8,128)(2,1)S(1)}, bf16[1024,128]{1,0:T(8,128)(2,1)S(1)}, u32[]{:S(2)}, u32[]{:S(2)}) collective-permute-start(bf16[1024,128]{1,0:T(8,128)(2,1)S(1)} %collective-permute-done.16.refs_10_), channel_id=1, source_target_pairs={{0,8},{8,16},{16,24},{24,28},{28,20},{20,12},{12,4},{4,0},{1,9},{9... | collective-permute-start | bytes 786440 | tf_op jit(solution)/shard_map/ppermute | solution.py:53
  113.7 2.1 %collective-permute-done.29.refs_7_.refs_25_.refs_23_ = bf16[336,256]{1,0:T(8,128)(2,1)S(1)} collective-permute-done((bf16[336,256]{1,0:T(8,128)(2,1)S(1)}, bf16[336,256]{1,0:T(8,128)(2,1)S(1)}, u32[]{:S(2)}, u32[]{:S(2)}) %collective-permute-start.29) | collective-permute-done | bytes 172064 | tf_op jit(solution)/shard_map/ppermute | solution.py:53
  115.8 0.5 collective-permute-start.47
  116.3 1.2 collective-permute-done.30.refs_8_.refs_26_.refs_24_
  117.5 0.5 collective-permute-start.39
  118.0 0.9 collective-permute-done.38.refs_16_.refs_34_.refs_32_
  119.2 0.7 sums.1
  119.9 0.5 collective-permute-start.48
  120.4 0.7 collective-permute-done.46.refs_14_
  121.1 1.5 %collective-permute-done.47.refs_15_ = bf16[1024,128]{1,0:T(8,128)(2,1)S(1)} collective-permute-done((bf16[1024,128]{1,0:T(8,128)(2,1)S(1)}, bf16[1024,128]{1,0:T(8,128)(2,1)S(1)}, u32[]{:S(2)}, u32[]{:S(2)}) %collective-permute-start.47) | collective-permute-done | bytes 262176 | tf_op jit(solution)/shard_map/ppermute | solution.py:53
  122.6 6.2 %gradients.1 = (bf16[1024,512]{1,0:T(8,128)(2,1)}, bf16[1024,512]{1,0:T(8,128)(2,1)}) custom-call(s32[1]{0:T(128)} %bitcast.p_ref, bf16[1024,128]{1,0:T(8,128)(2,1)S(1)} %get-tuple-element.79.refs_0_, bf16[1024,128]{1,0:T(8,128)(2,1)S(1)} %get-tuple-element.97.refs_1_, bf16[1024,128]{1,0:T(8,128)(2,1)S(1)} %collective-permute-done.14.refs_2_, ...), custom_call_target="tpu_custom_call" | custom-call | flops 4294967296 | bytes 11796480 | tf_op jit(solution)/shard_map/gradients/pallas_call | solution.py:372
  128.9 0.6 reduce
  129.4 0.7 join.1
  (75 shorter events, 3.9 us)
Async XLA Ops:
  0.6 0.7 copy-start.5
  1.3 0.7 copy-start.6
  3.5 5.1 %collective-permute-start = (bf16[144,1024]{1,0:T(8,128)(2,1)S(1)}, bf16[144,1024]{1,0:T(8,128)(2,1)S(1)}, u32[]{:S(2)}, u32[]{:S(2)}) collective-permute-start(bf16[144,1024]{1,0:T(8,128)(2,1)S(1)} %get-tuple-element.58.refs_0_), channel_id=1, source_target_pairs={{0,1},{1,0},{2,3},{3,2},{4,5},{5,4},{6,7},{7,6},{8,9},{9,8},{10,11... | collective-permute-start | bytes 884744 | tf_op jit(solution)/shard_map/ppermute | solution.py:20
  5.5 3.1 %collective-permute-start.1 = (bf16[144,1024]{1,0:T(8,128)(2,1)S(1)}, bf16[144,1024]{1,0:T(8,128)(2,1)S(1)}, u32[]{:S(2)}, u32[]{:S(2)}) collective-permute-start(bf16[144,1024]{1,0:T(8,128)(2,1)S(1)} %get-tuple-element.59.refs_1_.refs_0_), channel_id=1, source_target_pairs={{0,1},{1,0},{2,3},{3,2},{4,5},{5,4},{6,7},{7,6},{8,9},{9,8},{10,11... | collective-permute-start | bytes 884744 | tf_op jit(solution)/shard_map/ppermute | solution.py:20
  5.6 10.8 %collective-permute-start.7 = (bf16[144,1024]{1,0:T(8,128)(2,1)S(1)}, bf16[144,1024]{1,0:T(8,128)(2,1)S(1)}, u32[]{:S(2)}, u32[]{:S(2)}) collective-permute-start(bf16[144,1024]{1,0:T(8,128)(2,1)S(1)} %get-tuple-element.58.refs_0_), channel_id=1, source_target_pairs={{0,2},{1,3},{2,0},{3,1},{4,6},{5,7},{6,4},{7,5},{8,10},{9,11},{10,... | collective-permute-start | bytes 884744 | tf_op jit(solution)/shard_map/ppermute | solution.py:20
  8.6 13.6 %collective-permute-start.2 = (bf16[144,1024]{1,0:T(8,128)(2,1)S(1)}, bf16[144,1024]{1,0:T(8,128)(2,1)S(1)}, u32[]{:S(2)}, u32[]{:S(2)}) collective-permute-start(bf16[144,1024]{1,0:T(8,128)(2,1)S(1)} %get-tuple-element.59.refs_1_.refs_0_), channel_id=1, source_target_pairs={{0,2},{1,3},{2,0},{3,1},{4,6},{5,7},{6,4},{7,5},{8,10},{9,11},{10,... | collective-permute-start | bytes 884744 | tf_op jit(solution)/shard_map/ppermute | solution.py:20
  16.4 6.4 %collective-permute-start.8 = (bf16[144,1024]{1,0:T(8,128)(2,1)S(1)}, bf16[144,1024]{1,0:T(8,128)(2,1)S(1)}, u32[]{:S(2)}, u32[]{:S(2)}) collective-permute-start(bf16[144,1024]{1,0:T(8,128)(2,1)S(1)} %collective-permute-done.7.refs_0_.refs_1_), channel_id=1, source_target_pairs={{0,1},{1,0},{2,3},{3,2},{4,5},{5,4},{6,7},{7,6},{8,9},{9,8},{10,11... | collective-permute-start | bytes 884744 | tf_op jit(solution)/shard_map/ppermute | solution.py:20
  22.2 5.1 %collective-permute-start.3 = (bf16[144,1024]{1,0:T(8,128)(2,1)S(1)}, bf16[144,1024]{1,0:T(8,128)(2,1)S(1)}, u32[]{:S(2)}, u32[]{:S(2)}) collective-permute-start(bf16[144,1024]{1,0:T(8,128)(2,1)S(1)} %collective-permute-done.2.refs_0_.refs_1_), channel_id=1, source_target_pairs={{0,1},{1,0},{2,3},{3,2},{4,5},{5,4},{6,7},{7,6},{8,9},{9,8},{10,11... | collective-permute-start | bytes 884744 | tf_op jit(solution)/shard_map/ppermute | solution.py:20
  24.8 6.0 %collective-permute-start.10 = (bf16[128,512]{1,0:T(8,128)(2,1)S(1)}, bf16[128,512]{1,0:T(8,128)(2,1)S(1)}, u32[]{:S(2)}, u32[]{:S(2)}) collective-permute-start(bf16[128,512]{1,0:T(8,128)(2,1)S(1)} %attend0.1.refs_0_), channel_id=1, source_target_pairs={{0,2},{1,3},{2,0},{3,1},{4,6},{5,7},{6,4},{7,5},{8,10},{9,11},{10,... | collective-permute-start | bytes 393224 | tf_op jit(solution)/shard_map/ppermute | solution.py:20
  27.2 7.8 %copy-start = (bf16[2048,1024]{1,0:T(8,128)(2,1)S(1)}, bf16[2048,1024]{1,0:T(8,128)(2,1)}, u32[]{:S(2)}) copy-start(bf16[2048,1024]{1,0:T(8,128)(2,1)} %refs_4_.5) | copy-start | bytes 12582916
  27.2 7.8 %copy-start.1 = (bf16[1024,512]{1,0:T(8,128)(2,1)S(1)}, bf16[1024,512]{1,0:T(8,128)(2,1)}, u32[]{:S(2)}) copy-start(bf16[1024,512]{1,0:T(8,128)(2,1)} %policy_ref.3) | copy-start | bytes 3145732
  27.2 7.8 %copy-start.2 = (bf16[1024,512]{1,0:T(8,128)(2,1)S(1)}, bf16[1024,512]{1,0:T(8,128)(2,1)}, u32[]{:S(2)}) copy-start(bf16[1024,512]{1,0:T(8,128)(2,1)} %value_ref.3) | copy-start | bytes 3145732
  27.2 7.8 %copy-start.4 = (f32[1024]{0:T(1024)S(1)}, f32[1024]{0:T(1024)}, u32[]{:S(2)}) copy-start(f32[1024]{0:T(1024)} %param.27) | copy-start | bytes 12292
  29.3 5.7 %collective-permute-start.5 = (bf16[128,512]{1,0:T(8,128)(2,1)S(1)}, bf16[128,512]{1,0:T(8,128)(2,1)S(1)}, u32[]{:S(2)}, u32[]{:S(2)}) collective-permute-start(bf16[128,512]{1,0:T(8,128)(2,1)S(1)} %attend1.1.refs_0_), channel_id=1, source_target_pairs={{0,2},{1,3},{2,0},{3,1},{4,6},{5,7},{6,4},{7,5},{8,10},{9,11},{10,... | collective-permute-start | bytes 393224 | tf_op jit(solution)/shard_map/ppermute | solution.py:20
  29.6 5.4 %collective-permute-start.9 = (bf16[128,512]{1,0:T(8,128)(2,1)S(1)}, bf16[128,512]{1,0:T(8,128)(2,1)S(1)}, u32[]{:S(2)}, u32[]{:S(2)}) collective-permute-start(bf16[128,512]{1,0:T(8,128)(2,1)S(1)} %attend0.1.refs_0_), channel_id=1, source_target_pairs={{0,1},{1,0},{2,3},{3,2},{4,5},{5,4},{6,7},{7,6},{8,9},{9,8},{10,11... | collective-permute-start | bytes 393224 | tf_op jit(solution)/shard_map/ppermute | solution.py:20
  30.8 4.2 %collective-permute-start.11 = (bf16[128,512]{1,0:T(8,128)(2,1)S(1)}, bf16[128,512]{1,0:T(8,128)(2,1)S(1)}, u32[]{:S(2)}, u32[]{:S(2)}) collective-permute-start(bf16[128,512]{1,0:T(8,128)(2,1)S(1)} %collective-permute-done.10.refs_2_), channel_id=1, source_target_pairs={{0,1},{1,0},{2,3},{3,2},{4,5},{5,4},{6,7},{7,6},{8,9},{9,8},{10,11... | collective-permute-start | bytes 393224 | tf_op jit(solution)/shard_map/ppermute | solution.py:20
  30.8 8.7 %collective-permute-start.4 = (bf16[128,512]{1,0:T(8,128)(2,1)S(1)}, bf16[128,512]{1,0:T(8,128)(2,1)S(1)}, u32[]{:S(2)}, u32[]{:S(2)}) collective-permute-start(bf16[128,512]{1,0:T(8,128)(2,1)S(1)} %attend1.1.refs_0_), channel_id=1, source_target_pairs={{0,1},{1,0},{2,3},{3,2},{4,5},{5,4},{6,7},{7,6},{8,9},{9,8},{10,11... | collective-permute-start | bytes 393224 | tf_op jit(solution)/shard_map/ppermute | solution.py:20
  35.0 4.5 %collective-permute-start.6 = (bf16[128,512]{1,0:T(8,128)(2,1)S(1)}, bf16[128,512]{1,0:T(8,128)(2,1)S(1)}, u32[]{:S(2)}, u32[]{:S(2)}) collective-permute-start(bf16[128,512]{1,0:T(8,128)(2,1)S(1)} %collective-permute-done.5.refs_2_), channel_id=1, source_target_pairs={{0,1},{1,0},{2,3},{3,2},{4,5},{5,4},{6,7},{7,6},{8,9},{9,8},{10,11... | collective-permute-start | bytes 393224 | tf_op jit(solution)/shard_map/ppermute | solution.py:20
  37.5 8.7 %collective-permute-start.14 = (bf16[1024,128]{1,0:T(8,128)(2,1)S(1)}, bf16[1024,128]{1,0:T(8,128)(2,1)S(1)}, u32[]{:S(2)}, u32[]{:S(2)}) collective-permute-start(bf16[1024,128]{1,0:T(8,128)(2,1)S(1)} %get-tuple-element.79.refs_0_), channel_id=1, source_target_pairs={{0,8},{8,16},{16,24},{24,28},{28,20},{20,12},{12,4},{4,0},{1,9},{9... | collective-permute-start | bytes 786440 | tf_op jit(solution)/shard_map/ppermute | solution.py:53
  39.1 8.7 %collective-permute-start.17 = (bf16[1024,128]{1,0:T(8,128)(2,1)S(1)}, bf16[1024,128]{1,0:T(8,128)(2,1)S(1)}, u32[]{:S(2)}, u32[]{:S(2)}) collective-permute-start(bf16[1024,128]{1,0:T(8,128)(2,1)S(1)} %get-tuple-element.79.refs_0_), channel_id=1, source_target_pairs={{0,4},{8,0},{16,8},{24,16},{28,24},{20,28},{12,20},{4,12},{1,5},{9... | collective-permute-start | bytes 786440 | tf_op jit(solution)/shard_map/ppermute | solution.py:53
  39.5 18.2 %copy-start.9 = (bf16[512]{0:T(512)(128)(2,1)S(1)}, bf16[512]{0:T(512)(128)(2,1)}, u32[]{:S(2)}) copy-start(bf16[512]{0:T(512)(128)(2,1)} %param.31) | copy-start | bytes 3076
  39.5 22.9 %copy-start.3 = (bf16[512,256]{1,0:T(8,128)(2,1)S(1)}, bf16[512,256]{1,0:T(8,128)(2,1)}, u32[]{:S(2)}) copy-start(bf16[512,256]{1,0:T(8,128)(2,1)} %policy_out_ref.1) | copy-start | bytes 786436
  39.5 22.9 %copy-start.7 = (s32[256]{0:T(256)S(1)}, s32[256]{0:T(256)}, u32[]{:S(2)}) copy-start(s32[256]{0:T(256)} %param.32) | copy-start | bytes 3076
  39.5 22.9 %copy-start.8 = (f32[256]{0:T(256)S(1)}, f32[256]{0:T(256)}, u32[]{:S(2)}) copy-start(f32[256]{0:T(256)} %param.33) | copy-start | bytes 3076
  42.0 6.2 %collective-permute-start.12 = (bf16[256,512]{1,0:T(8,128)(2,1)S(1)}, bf16[256,512]{1,0:T(8,128)(2,1)S(1)}, u32[]{:S(2)}, u32[]{:S(2)}) collective-permute-start(bf16[256,512]{1,0:T(8,128)(2,1)S(1)} %get-tuple-element.78), channel_id=1, source_target_pairs={{0,1},{1,0},{2,3},{3,2},{4,5},{5,4},{6,7},{7,6},{8,9},{9,8},{10,11... | collective-permute-start | bytes 786440 | tf_op jit(solution)/shard_map/ppermute | solution.py:20
  46.2 7.9 %collective-permute-start.15 = (bf16[1024,128]{1,0:T(8,128)(2,1)S(1)}, bf16[1024,128]{1,0:T(8,128)(2,1)S(1)}, u32[]{:S(2)}, u32[]{:S(2)}) collective-permute-start(bf16[1024,128]{1,0:T(8,128)(2,1)S(1)} %collective-permute-done.14.refs_2_), channel_id=1, source_target_pairs={{0,8},{8,16},{16,24},{24,28},{28,20},{20,12},{12,4},{4,0},{1,9},{9... | collective-permute-start | bytes 786440 | tf_op jit(solution)/shard_map/ppermute | solution.py:53
  47.8 7.9 %collective-permute-start.18 = (bf16[1024,128]{1,0:T(8,128)(2,1)S(1)}, bf16[1024,128]{1,0:T(8,128)(2,1)S(1)}, u32[]{:S(2)}, u32[]{:S(2)}) collective-permute-start(bf16[1024,128]{1,0:T(8,128)(2,1)S(1)} %collective-permute-done.17.refs_4_), channel_id=1, source_target_pairs={{0,4},{8,0},{16,8},{24,16},{28,24},{20,28},{12,20},{4,12},{1,5},{9... | collective-permute-start | bytes 786440 | tf_op jit(solution)/shard_map/ppermute | solution.py:53
  48.3 12.7 %collective-permute-start.13 = (bf16[256,512]{1,0:T(8,128)(2,1)S(1)}, bf16[256,512]{1,0:T(8,128)(2,1)S(1)}, u32[]{:S(2)}, u32[]{:S(2)}) collective-permute-start(bf16[256,512]{1,0:T(8,128)(2,1)S(1)} %add_convert_fusion.mine_ref), channel_id=1, source_target_pairs={{0,2},{1,3},{2,0},{3,1},{4,6},{5,7},{6,4},{7,5},{8,10},{9,11},{10,... | collective-permute-start | bytes 786440 | tf_op jit(solution)/shard_map/ppermute | solution.py:20
  54.1 7.0 %collective-permute-start.16 = (bf16[1024,128]{1,0:T(8,128)(2,1)S(1)}, bf16[1024,128]{1,0:T(8,128)(2,1)S(1)}, u32[]{:S(2)}, u32[]{:S(2)}) collective-permute-start(bf16[1024,128]{1,0:T(8,128)(2,1)S(1)} %collective-permute-done.15.refs_6_), channel_id=1, source_target_pairs={{0,8},{8,16},{16,24},{24,28},{28,20},{20,12},{12,4},{4,0},{1,9},{9... | collective-permute-start | bytes 786440 | tf_op jit(solution)/shard_map/ppermute | solution.py:53
  55.7 6.8 %collective-permute-start.19 = (bf16[1024,128]{1,0:T(8,128)(2,1)S(1)}, bf16[1024,128]{1,0:T(8,128)(2,1)S(1)}, u32[]{:S(2)}, u32[]{:S(2)}) collective-permute-start(bf16[1024,128]{1,0:T(8,128)(2,1)S(1)} %collective-permute-done.18.refs_8_), channel_id=1, source_target_pairs={{0,4},{8,0},{16,8},{24,16},{28,24},{20,28},{12,20},{4,12},{1,5},{9... | collective-permute-start | bytes 786440 | tf_op jit(solution)/shard_map/ppermute | solution.py:53
  56.2 1.2 collective-permute-start.20
  57.3 3.7 %collective-permute-start.21 = (f32[8,256]{1,0:T(8,128)S(1)}, f32[8,256]{1,0:T(8,128)S(1)}, u32[]{:S(2)}, u32[]{:S(2)}) collective-permute-start(f32[8,256]{1,0:T(8,128)S(1)} %add.14), channel_id=1, source_target_pairs={{0,2},{1,3},{2,0},{3,1},{4,6},{5,7},{6,4},{7,5},{8,10},{9,11},{10,... | collective-permute-start | bytes 24584 | tf_op jit(solution)/shard_map/ppermute | solution.py:20
  63.6 1.3 %collective-permute-start.22 = (bf16[64,512]{1,0:T(8,128)(2,1)S(1)}, bf16[64,512]{1,0:T(8,128)(2,1)S(1)}, u32[]{:S(2)}, u32[]{:S(2)}) collective-permute-start(bf16[64,512]{1,0:T(8,128)(2,1)S(1)} %get-tuple-element.85), channel_id=1, source_target_pairs={{0,1},{1,0},{2,3},{3,2},{4,5},{5,4},{6,7},{7,6},{8,9},{9,8},{10,11... | collective-permute-start | bytes 196616 | tf_op jit(solution)/shard_map/ppermute | solution.py:20
  65.0 11.0 %collective-permute-start.23 = (bf16[336,512]{1,0:T(8,128)(2,1)S(1)}, bf16[336,512]{1,0:T(8,128)(2,1)S(1)}, u32[]{:S(2)}, u32[]{:S(2)}) collective-permute-start(bf16[336,512]{1,0:T(8,128)(2,1)S(1)} %select_dynamic-update-slice_fusion.refs_0_.refs_18_.refs_16_), channel_id=1, source_target_pairs={{0,8},{8,16},{16,24},{24,28},{28,20},{20,12},{12,4},{4,0},{1,9},{9... | collective-permute-start | bytes 1032200 | tf_op jit(solution)/shard_map/ppermute | solution.py:53
  66.6 17.0 %collective-permute-start.24 = (bf16[336,512]{1,0:T(8,128)(2,1)S(1)}, bf16[336,512]{1,0:T(8,128)(2,1)S(1)}, u32[]{:S(2)}, u32[]{:S(2)}) collective-permute-start(bf16[336,512]{1,0:T(8,128)(2,1)S(1)} %select_dynamic-update-slice_fusion.refs_0_.refs_18_.refs_16_), channel_id=1, source_target_pairs={{0,4},{8,0},{16,8},{24,16},{28,24},{20,28},{12,20},{4,12},{1,5},{9... | collective-permute-start | bytes 1032200 | tf_op jit(solution)/shard_map/ppermute | solution.py:53
  67.0 14.5 %collective-permute-start.40 = (bf16[1024,128]{1,0:T(8,128)(2,1)S(1)}, bf16[1024,128]{1,0:T(8,128)(2,1)S(1)}, u32[]{:S(2)}, u32[]{:S(2)}) collective-permute-start(bf16[1024,128]{1,0:T(8,128)(2,1)S(1)} %get-tuple-element.97.refs_1_), channel_id=1, source_target_pairs={{0,8},{8,16},{16,24},{24,28},{28,20},{20,12},{12,4},{4,0},{1,9},{9... | collective-permute-start | bytes 786440 | tf_op jit(solution)/shard_map/ppermute | solution.py:53
  68.6 14.5 %collective-permute-start.41 = (bf16[1024,128]{1,0:T(8,128)(2,1)S(1)}, bf16[1024,128]{1,0:T(8,128)(2,1)S(1)}, u32[]{:S(2)}, u32[]{:S(2)}) collective-permute-start(bf16[1024,128]{1,0:T(8,128)(2,1)S(1)} %get-tuple-element.97.refs_1_), channel_id=1, source_target_pairs={{0,4},{8,0},{16,8},{24,16},{28,24},{20,28},{12,20},{4,12},{1,5},{9... | collective-permute-start | bytes 786440 | tf_op jit(solution)/shard_map/ppermute | solution.py:53
  75.9 19.9 %collective-permute-start.25 = (bf16[336,512]{1,0:T(8,128)(2,1)S(1)}, bf16[336,512]{1,0:T(8,128)(2,1)S(1)}, u32[]{:S(2)}, u32[]{:S(2)}) collective-permute-start(bf16[336,512]{1,0:T(8,128)(2,1)S(1)} %collective-permute-done.23.refs_1_.refs_19_.refs_17_), channel_id=1, source_target_pairs={{0,8},{8,16},{16,24},{24,28},{28,20},{20,12},{12,4},{4,0},{1,9},{9... | collective-permute-start | bytes 1032200 | tf_op jit(solution)/shard_map/ppermute | solution.py:53
  81.5 12.2 %collective-permute-start.42 = (bf16[1024,128]{1,0:T(8,128)(2,1)S(1)}, bf16[1024,128]{1,0:T(8,128)(2,1)S(1)}, u32[]{:S(2)}, u32[]{:S(2)}) collective-permute-start(bf16[1024,128]{1,0:T(8,128)(2,1)S(1)} %collective-permute-done.40.refs_3_), channel_id=1, source_target_pairs={{0,8},{8,16},{16,24},{24,28},{28,20},{20,12},{12,4},{4,0},{1,9},{9... | collective-permute-start | bytes 786440 | tf_op jit(solution)/shard_map/ppermute | solution.py:53
  83.1 12.2 %collective-permute-start.43 = (bf16[1024,128]{1,0:T(8,128)(2,1)S(1)}, bf16[1024,128]{1,0:T(8,128)(2,1)S(1)}, u32[]{:S(2)}, u32[]{:S(2)}) collective-permute-start(bf16[1024,128]{1,0:T(8,128)(2,1)S(1)} %collective-permute-done.41.refs_5_), channel_id=1, source_target_pairs={{0,4},{8,0},{16,8},{24,16},{28,24},{20,28},{12,20},{4,12},{1,5},{9... | collective-permute-start | bytes 786440 | tf_op jit(solution)/shard_map/ppermute | solution.py:53
  83.6 13.4 %collective-permute-start.26 = (bf16[336,512]{1,0:T(8,128)(2,1)S(1)}, bf16[336,512]{1,0:T(8,128)(2,1)S(1)}, u32[]{:S(2)}, u32[]{:S(2)}) collective-permute-start(bf16[336,512]{1,0:T(8,128)(2,1)S(1)} %collective-permute-done.24.refs_2_.refs_20_.refs_18_), channel_id=1, source_target_pairs={{0,4},{8,0},{16,8},{24,16},{28,24},{20,28},{12,20},{4,12},{1,5},{9... | collective-permute-start | bytes 1032200 | tf_op jit(solution)/shard_map/ppermute | solution.py:53
  84.0 14.5 %collective-permute-start.31 = (bf16[336,512]{1,0:T(8,128)(2,1)S(1)}, bf16[336,512]{1,0:T(8,128)(2,1)S(1)}, u32[]{:S(2)}, u32[]{:S(2)}) collective-permute-start(bf16[336,512]{1,0:T(8,128)(2,1)S(1)} %select_dynamic-update-slice_fusion.refs_0_.refs_18_.refs_16_), channel_id=1, source_target_pairs={{0,1},{1,0},{2,3},{3,2},{4,5},{5,4},{6,7},{7,6},{8,9},{9,8},{10,11... | collective-permute-start | bytes 1032200 | tf_op jit(solution)/shard_map/ppermute | solution.py:20
  93.8 9.2 %collective-permute-start.44 = (bf16[1024,128]{1,0:T(8,128)(2,1)S(1)}, bf16[1024,128]{1,0:T(8,128)(2,1)S(1)}, u32[]{:S(2)}, u32[]{:S(2)}) collective-permute-start(bf16[1024,128]{1,0:T(8,128)(2,1)S(1)} %collective-permute-done.42.refs_7_), channel_id=1, source_target_pairs={{0,8},{8,16},{16,24},{24,28},{28,20},{20,12},{12,4},{4,0},{1,9},{9... | collective-permute-start | bytes 786440 | tf_op jit(solution)/shard_map/ppermute | solution.py:53
  95.3 9.2 %collective-permute-start.45 = (bf16[1024,128]{1,0:T(8,128)(2,1)S(1)}, bf16[1024,128]{1,0:T(8,128)(2,1)S(1)}, u32[]{:S(2)}, u32[]{:S(2)}) collective-permute-start(bf16[1024,128]{1,0:T(8,128)(2,1)S(1)} %collective-permute-done.43.refs_9_), channel_id=1, source_target_pairs={{0,4},{8,0},{16,8},{24,16},{28,24},{20,28},{12,20},{4,12},{1,5},{9... | collective-permute-start | bytes 786440 | tf_op jit(solution)/shard_map/ppermute | solution.py:53
  95.8 8.8 %collective-permute-start.32 = (bf16[336,512]{1,0:T(8,128)(2,1)S(1)}, bf16[336,512]{1,0:T(8,128)(2,1)S(1)}, u32[]{:S(2)}, u32[]{:S(2)}) collective-permute-start(bf16[336,512]{1,0:T(8,128)(2,1)S(1)} %collective-permute-done.23.refs_1_.refs_19_.refs_17_), channel_id=1, source_target_pairs={{0,1},{1,0},{2,3},{3,2},{4,5},{5,4},{6,7},{7,6},{8,9},{9,8},{10,11... | collective-permute-start | bytes 1032200 | tf_op jit(solution)/shard_map/ppermute | solution.py:20
  97.0 11.7 %collective-permute-start.27 = (bf16[336,512]{1,0:T(8,128)(2,1)S(1)}, bf16[336,512]{1,0:T(8,128)(2,1)S(1)}, u32[]{:S(2)}, u32[]{:S(2)}) collective-permute-start(bf16[336,512]{1,0:T(8,128)(2,1)S(1)} %collective-permute-done.25.refs_3_.refs_21_.refs_19_), channel_id=1, source_target_pairs={{0,8},{8,16},{16,24},{24,28},{28,20},{20,12},{12,4},{4,0},{1,9},{9... | collective-permute-start | bytes 1032200 | tf_op jit(solution)/shard_map/ppermute | solution.py:53
  98.5 11.4 %collective-permute-start.28 = (bf16[336,512]{1,0:T(8,128)(2,1)S(1)}, bf16[336,512]{1,0:T(8,128)(2,1)S(1)}, u32[]{:S(2)}, u32[]{:S(2)}) collective-permute-start(bf16[336,512]{1,0:T(8,128)(2,1)S(1)} %collective-permute-done.26.refs_4_.refs_22_.refs_20_), channel_id=1, source_target_pairs={{0,4},{8,0},{16,8},{24,16},{28,24},{20,28},{12,20},{4,12},{1,5},{9... | collective-permute-start | bytes 1032200 | tf_op jit(solution)/shard_map/ppermute | solution.py:53
  103.0 8.6 %collective-permute-start.33 = (bf16[336,512]{1,0:T(8,128)(2,1)S(1)}, bf16[336,512]{1,0:T(8,128)(2,1)S(1)}, u32[]{:S(2)}, u32[]{:S(2)}) collective-permute-start(bf16[336,512]{1,0:T(8,128)(2,1)S(1)} %collective-permute-done.24.refs_2_.refs_20_.refs_18_), channel_id=1, source_target_pairs={{0,1},{1,0},{2,3},{3,2},{4,5},{5,4},{6,7},{7,6},{8,9},{9,8},{10,11... | collective-permute-start | bytes 1032200 | tf_op jit(solution)/shard_map/ppermute | solution.py:20
  104.6 7.5 %collective-permute-start.34 = (bf16[336,512]{1,0:T(8,128)(2,1)S(1)}, bf16[336,512]{1,0:T(8,128)(2,1)S(1)}, u32[]{:S(2)}, u32[]{:S(2)}) collective-permute-start(bf16[336,512]{1,0:T(8,128)(2,1)S(1)} %collective-permute-done.25.refs_3_.refs_21_.refs_19_), channel_id=1, source_target_pairs={{0,1},{1,0},{2,3},{3,2},{4,5},{5,4},{6,7},{7,6},{8,9},{9,8},{10,11... | collective-permute-start | bytes 1032200 | tf_op jit(solution)/shard_map/ppermute | solution.py:20
  104.6 7.5 %collective-permute-start.35 = (bf16[336,512]{1,0:T(8,128)(2,1)S(1)}, bf16[336,512]{1,0:T(8,128)(2,1)S(1)}, u32[]{:S(2)}, u32[]{:S(2)}) collective-permute-start(bf16[336,512]{1,0:T(8,128)(2,1)S(1)} %collective-permute-done.26.refs_4_.refs_22_.refs_20_), channel_id=1, source_target_pairs={{0,1},{1,0},{2,3},{3,2},{4,5},{5,4},{6,7},{7,6},{8,9},{9,8},{10,11... | collective-permute-start | bytes 1032200 | tf_op jit(solution)/shard_map/ppermute | solution.py:20
  108.7 8.8 %collective-permute-start.36 = (bf16[336,512]{1,0:T(8,128)(2,1)S(1)}, bf16[336,512]{1,0:T(8,128)(2,1)S(1)}, u32[]{:S(2)}, u32[]{:S(2)}) collective-permute-start(bf16[336,512]{1,0:T(8,128)(2,1)S(1)} %collective-permute-done.27.refs_5_.refs_23_.refs_21_), channel_id=1, source_target_pairs={{0,1},{1,0},{2,3},{3,2},{4,5},{5,4},{6,7},{7,6},{8,9},{9,8},{10,11... | collective-permute-start | bytes 1032200 | tf_op jit(solution)/shard_map/ppermute | solution.py:20
  110.0 5.8 %collective-permute-start.29 = (bf16[336,256]{1,0:T(8,128)(2,1)S(1)}, bf16[336,256]{1,0:T(8,128)(2,1)S(1)}, u32[]{:S(2)}, u32[]{:S(2)}) collective-permute-start(bf16[336,256]{1,0:T(8,128)(2,1)S(1)} %slice.12), channel_id=1, source_target_pairs={{0,8},{8,16},{16,24},{24,28},{28,20},{20,12},{12,4},{4,0},{1,9},{9... | collective-permute-start | bytes 516104 | tf_op jit(solution)/shard_map/ppermute | solution.py:53
  111.6 5.9 %collective-permute-start.30 = (bf16[336,256]{1,0:T(8,128)(2,1)S(1)}, bf16[336,256]{1,0:T(8,128)(2,1)S(1)}, u32[]{:S(2)}, u32[]{:S(2)}) collective-permute-start(bf16[336,256]{1,0:T(8,128)(2,1)S(1)} %slice.13), channel_id=1, source_target_pairs={{0,4},{8,0},{16,8},{24,16},{28,24},{20,28},{12,20},{4,12},{1,5},{9... | collective-permute-start | bytes 516104 | tf_op jit(solution)/shard_map/ppermute | solution.py:53
  112.1 5.9 %collective-permute-start.37 = (bf16[336,512]{1,0:T(8,128)(2,1)S(1)}, bf16[336,512]{1,0:T(8,128)(2,1)S(1)}, u32[]{:S(2)}, u32[]{:S(2)}) collective-permute-start(bf16[336,512]{1,0:T(8,128)(2,1)S(1)} %collective-permute-done.28.refs_6_.refs_24_.refs_22_), channel_id=1, source_target_pairs={{0,1},{1,0},{2,3},{3,2},{4,5},{5,4},{6,7},{7,6},{8,9},{9,8},{10,11... | collective-permute-start | bytes 1032200 | tf_op jit(solution)/shard_map/ppermute | solution.py:20
  112.1 9.1 %collective-permute-start.46 = (bf16[1024,128]{1,0:T(8,128)(2,1)S(1)}, bf16[1024,128]{1,0:T(8,128)(2,1)S(1)}, u32[]{:S(2)}, u32[]{:S(2)}) collective-permute-start(bf16[1024,128]{1,0:T(8,128)(2,1)S(1)} %collective-permute-done.16.refs_10_), channel_id=1, source_target_pairs={{0,8},{8,16},{16,24},{24,28},{28,20},{20,12},{12,4},{4,0},{1,9},{9... | collective-permute-start | bytes 786440 | tf_op jit(solution)/shard_map/ppermute | solution.py:53
  115.8 6.8 %collective-permute-start.47 = (bf16[1024,128]{1,0:T(8,128)(2,1)S(1)}, bf16[1024,128]{1,0:T(8,128)(2,1)S(1)}, u32[]{:S(2)}, u32[]{:S(2)}) collective-permute-start(bf16[1024,128]{1,0:T(8,128)(2,1)S(1)} %collective-permute-done.45.refs_13_), channel_id=1, source_target_pairs={{0,4},{8,0},{16,8},{24,16},{28,24},{20,28},{12,20},{4,12},{1,5},{9... | collective-permute-start | bytes 786440 | tf_op jit(solution)/shard_map/ppermute | solution.py:53
  117.5 1.4 %collective-permute-start.38 = (bf16[336,256]{1,0:T(8,128)(2,1)S(1)}, bf16[336,256]{1,0:T(8,128)(2,1)S(1)}, u32[]{:S(2)}, u32[]{:S(2)}) collective-permute-start(bf16[336,256]{1,0:T(8,128)(2,1)S(1)} %collective-permute-done.29.refs_7_.refs_25_.refs_23_), channel_id=1, source_target_pairs={{0,1},{1,0},{2,3},{3,2},{4,5},{5,4},{6,7},{7,6},{8,9},{9,8},{10,11... | collective-permute-start | bytes 516104 | tf_op jit(solution)/shard_map/ppermute | solution.py:20
  117.5 1.6 %collective-permute-start.39 = (bf16[336,256]{1,0:T(8,128)(2,1)S(1)}, bf16[336,256]{1,0:T(8,128)(2,1)S(1)}, u32[]{:S(2)}, u32[]{:S(2)}) collective-permute-start(bf16[336,256]{1,0:T(8,128)(2,1)S(1)} %collective-permute-done.30.refs_8_.refs_26_.refs_24_), channel_id=1, source_target_pairs={{0,1},{1,0},{2,3},{3,2},{4,5},{5,4},{6,7},{7,6},{8,9},{9,8},{10,11... | collective-permute-start | bytes 516104 | tf_op jit(solution)/shard_map/ppermute | solution.py:20
  119.9 9.6 %collective-permute-start.48 = (bf16[256,256]{1,0:T(8,128)(2,1)S(1)}, bf16[256,256]{1,0:T(8,128)(2,1)S(1)}, u32[]{:S(2)}, u32[]{:S(2)}) collective-permute-start(bf16[256,256]{1,0:T(8,128)(2,1)S(1)} %get-tuple-element.106.refs_0_), channel_id=1, source_target_pairs={{0,2},{1,3},{2,0},{3,1},{4,6},{5,7},{6,4},{7,5},{8,10},{9,11},{10,... | collective-permute-start | bytes 393224 | tf_op jit(solution)/shard_map/ppermute | solution.py:20
